TPU v7x, 256 devices: a whole 4x4x8 slice. The times are simulated.
256 devices in a mesh: task: 2 (over x_lo), dp: 16 (over z, core), mp: 8 (over x_hi, y).
Axes of the slice: x: 4 (x_hi: 2, x_lo: 2; x = x_hi * 2 + x_lo), y: 4, z: 8, core: 2. Of those that a mesh axis runs over, the one named last changes fastest.
Arguments:
- deltas: bfloat16 [6, 4096, 4608], P('task', 'dp', 'mp'), may hold values from -400 to 400, as said below
- fishers: bfloat16 [6, 4096, 4608], P('task', 'dp', 'mp'), may hold values from 0.0009994507 to 1
Outputs:
- merged_out: float32 [4096, 4608], P('dp', 'mp')
Inputs may be any that keep to these rules, and one draw needn't show every extreme that they name: `deltas`: Real-valued weight differences.
All inputs are finite; a program needn't handle non-finite values.
Results may differ from a plain program's by a relative error of at most 0.0003.
Values sent between devices are 32-bit elements; how exact they have to be, the bound alone decides.
No kernel may reach another device: no remote copies, remote signals or barrier semaphores. Data moves between devices by JAX's collectives and lax.ppermute only.
A program may use at most 64 MiB of HBM per device.

v0:
```python
import functools

import jax
import jax.numpy as jnp
from jax import lax
from jax.sharding import Mesh
from jax.sharding import PartitionSpec as P

TASK_DP_MP = ("task", "dp_0", "dp_1", "mp_0", "mp_1")
DP = ("dp_0", "dp_1")
MP = ("mp_0", "mp_1")


def over_axes(array, axes):
    return functools.reduce(lax.psum, axes, array)


def cut_along(array, dim, size):
    before, after = (array.shape[:dim], array.shape[dim + 1 :])
    return jnp.moveaxis(array.reshape(*before, size, -1, *after), dim, 0)


def sum_at_owner(array, axis, dim):
    size = lax.axis_size(axis)
    tiles = lax.all_to_all(cut_along(array, dim, size), axis, 0, 0, tiled=True)
    return jnp.sum(tiles, axis=0)


def side_by_side(arrays, axis, dim, along):
    ends, at = ([], 0)
    for a in arrays[:-1]:
        at += a.shape[along]
        ends.append(at)
    both = jnp.concatenate(arrays, axis=along)
    return tuple(jnp.split(sum_at_owner(both, axis, dim), ends, axis=along))


def laid_out(tiles, dim):
    tiles = jnp.moveaxis(tiles, 0, dim)
    shape = tiles.shape
    return tiles.reshape(*shape[:dim], shape[dim] * shape[dim + 1], *shape[dim + 2 :])


def from_everyone(array, axis):
    size = lax.axis_size(axis)
    return lax.all_to_all(
        jnp.broadcast_to(array[None], (size, *array.shape)), axis, 0, 0, tiled=True
    )


def gathered_copies(array, axis, dim):
    return laid_out(from_everyone(array, axis), dim)


def task_squares(deltas):
    widened = deltas.astype(jnp.float32)
    own_sums = jnp.sum(widened * widened, axis=(1, 2))
    held_tasks = deltas.shape[0]
    slot_sums = jnp.zeros((held_tasks * lax.axis_size("task"),), jnp.float32)
    return lax.dynamic_update_slice(slot_sums, own_sums, (lax.axis_index("task") * held_tasks,))


def shards(deltas, fishers):
    weights = fishers.astype(jnp.float32)
    numerator = jnp.sum(weights * deltas.astype(jnp.float32), axis=0)
    denominator = jnp.sum(weights, axis=0)
    task_part = task_squares(deltas)
    task_sq = over_axes(task_part, TASK_DP_MP)
    numerator, denominator = side_by_side((numerator, denominator), "task", 0, 1)
    half_rows = numerator / denominator
    merged_part = jnp.sum(half_rows * half_rows)
    merged = gathered_copies(half_rows, "task", 0)
    merged_sq = over_axes(merged_part, TASK_DP_MP)
    target = jnp.mean(jnp.sqrt(task_sq + 1e-06))
    rescale = target / jnp.sqrt(merged_sq + 1e-06)
    return rescale * merged


def solution(mesh):
    torus = Mesh(
        mesh.devices.reshape(mesh.shape["task"], 8, 2, 2, 4),
        ("task", "dp_0", "dp_1", "mp_0", "mp_1"),
    )
    placed = (P("task", DP, MP), P("task", DP, MP))
    return jax.shard_map(shards, mesh=torus, in_specs=placed, out_specs=P(DP, MP), check_vma=False)
```

profile of v0, /device:TPU:4, one launch (start us, length us, event | category | flops | bytes accessed | tf_op | source)
XLA Modules:
  0.0 79.1 jit_solution(12822121947898683970)
XLA Ops:
  0.0 2.1 %fusion = (f32[3]{0:T(128)S(1)}, f32[256,576]{0,1:T(8,128)S(1)}, f32[256,576]{0,1:T(8,128)S(1)}) fusion(bf16[3,256,576]{1,2,0:T(8,128)(2,1)} %param.2, bf16[3,256,576]{1,2,0:T(8,128)(2,1)} %param.3), kind=kLoop, calls=%fused_computation.3 | loop fusion | flops 2801661 | bytes 2949132 | tf_op jit(solution)/shard_map/reduce_sum | solution.py:57
  2.1 0.1 copy_bitcast_fusion
  2.2 17.7 %all_to_all.10 = f32[2,128,1152]{1,2,0:T(8,128)S(1)} all-to-all(f32[2,128,1152]{1,2,0:T(8,128)S(1)} %copy_bitcast_fusion), channel_id=1, replica_groups=mesh['task'=2,'dp_0'=8,'dp_1'=2,'mp_0'=2,'mp_1'=4] {'task'}, dimensions={0} | all-to-all | bytes 2359296 | tf_op jit(solution)/shard_map/all_to_all | solution.py:25
  19.9 0.1 reduce_sum.58
  20.1 0.7 multiply_reduce_fusion
  20.7 0.9 %broadcast_in_dim.2 = f32[2,128,576]{1,2,0:T(8,128)} broadcast(f32[128,576]{0,1:T(8,128)S(1)} %get-tuple-element.19), dimensions={1,2} | broadcast | bytes 884736 | tf_op jit(solution)/shard_map/broadcast_in_dim | solution.py:47
  21.6 3.5 %all-to-all-start.1 = ((f32[2,128,576]{1,2,0:T(8,128)}), f32[2,128,576]{1,2,0:T(8,128)S(1)}, u32[]{:S(2)}, u32[]{:S(2)}) async-start(f32[2,128,576]{1,2,0:T(8,128)} %broadcast_in_dim.2), calls=%async_computation.1 | async-start | bytes 1179648 | tf_op jit(solution)/shard_map/all_to_all | solution.py:46
  25.1 0.2 dynamic_update_slice.3
  25.4 8.5 %all-reduce.4 = (f32[6]{0:T(128)S(1)}, f32[]{:T(128)}) all-reduce(f32[6]{0:T(128)S(1)} %dynamic_update_slice.3, f32[]{:T(128)} %get-tuple-element.18), channel_id=1, replica_groups=mesh['task'=2,'dp_0'=8,'dp_1'=2,'mp_0'=2,'mp_1'=4] {'task'}, use_global_device_ids=true, to_apply=%region_1.0 | all-reduce | flops 7 | bytes 56 | tf_op jit(solution)/shard_map/psum | solution.py:15
  33.8 20.6 %all-reduce = (f32[6]{0:T(128)S(1)}, f32[]{:T(128)}) all-reduce(f32[6]{0:T(128)S(1)} %get-tuple-element.16, f32[]{:T(128)} %get-tuple-element.17), channel_id=1, replica_groups=mesh['task'=2,'dp_0'=8,'dp_1'=2,'mp_0'=2,'mp_1'=4] {'dp_0'}, use_global_device_ids=true, to_apply=%region_2.0 | all-reduce | flops 7 | bytes 56 | tf_op jit(solution)/shard_map/psum | solution.py:15
  54.5 3.2 %all-reduce.3 = (f32[6]{0:T(128)S(1)}, f32[]{:T(128)}) all-reduce(f32[6]{0:T(128)S(1)} %get-tuple-element.8, f32[]{:T(128)} %get-tuple-element.9), channel_id=1, replica_groups=mesh['task'=2,'dp_0'=8,'dp_1'=2,'mp_0'=2,'mp_1'=4] {'dp_1'}, use_global_device_ids=true, to_apply=%region_3.0 | all-reduce | flops 7 | bytes 56 | tf_op jit(solution)/shard_map/psum | solution.py:15
  57.6 7.1 %all-reduce.2 = (f32[6]{0:T(128)S(1)}, f32[]{:T(128)}) all-reduce(f32[6]{0:T(128)S(1)} %get-tuple-element.14, f32[]{:T(128)} %get-tuple-element.15), channel_id=1, replica_groups=mesh['task'=2,'dp_0'=8,'dp_1'=2,'mp_0'=2,'mp_1'=4] {'mp_0'}, use_global_device_ids=true, to_apply=%region_4.0 | all-reduce | flops 7 | bytes 56 | tf_op jit(solution)/shard_map/psum | solution.py:15
  64.7 11.4 %all-reduce.1 = (f32[6]{0:T(128)S(1)}, f32[]{:T(128)}) all-reduce(f32[6]{0:T(128)S(1)} %get-tuple-element.12, f32[]{:T(128)} %get-tuple-element.13), channel_id=1, replica_groups=mesh['task'=2,'dp_0'=8,'dp_1'=2,'mp_0'=2,'mp_1'=4] {'mp_1'}, use_global_device_ids=true, to_apply=%region_5.0 | all-reduce | flops 7 | bytes 56 | tf_op jit(solution)/shard_map/psum | solution.py:15
  76.8 0.7 sqrt_reduce_fusion
  78.2 0.0 all-to-all-done.1
  78.2 0.9 %copy_bitcast_fusion.1 = f32[256,576]{0,1:T(8,128)} fusion(f32[2,128,576]{1,2,0:T(8,128)S(1)} %all-to-all-done.1, f32[]{:T(128)S(6)} %div.11), kind=kLoop, calls=%fused_computation.7 | loop fusion | flops 147456 | bytes 1179652 | tf_op jit(solution)/shard_map/mul | solution.py:76
  (1 shorter events, 0.0 us)
Async XLA Ops:
  21.6 56.6 %all-to-all-start.1 = ((f32[2,128,576]{1,2,0:T(8,128)}), f32[2,128,576]{1,2,0:T(8,128)S(1)}, u32[]{:S(2)}, u32[]{:S(2)}) async-start(f32[2,128,576]{1,2,0:T(8,128)} %broadcast_in_dim.2), calls=%async_computation.1 | async-start | bytes 1179648 | tf_op jit(solution)/shard_map/all_to_all | solution.py:46
where the time goes:
time: 79.4 us; the launch traced here: 79.1 us
  blocking collectives  68.5 us (86%)
  other arithmetic  4.52 us (6%)
  starting transfers between devices  3.5 us (4%)
  between operations  1.48 us (2%)
  local copies, waits for them, and re-layouts  1.1 us (1%)
    psum x5, blocking collectives, over_axes(): return functools.reduce(lax.psum, axes, array)  50.7 us
    all_to_all x1, blocking collectives, sum_at_owner(): tiles = lax.all_to_all(cut_along(array, dim, size), axis, 0, 0, tiled=True)  17.7 us
    all_to_all x1, starting transfers between devices, from_everyone(): lax.all_to_all(jnp.broadcast_to(array[None], (size, *array.shape)), axis,...  3.5 us
    reduce_sum x1, other arithmetic, task_squares(): own_sums = jnp.sum(widened * widened, axis=(1, 2))  2.1 us
  transfers between devices with their start and end apart: 1, of which 0 were waited for; matrix products, arithmetic and copies ran while one was open for 1% of the time, Pallas kernels for 0%

commit v1 on v0

v1 whole, which is shorter than its diff:
```python
import jax
import jax.numpy as jnp
from jax import lax
from jax.sharding import PartitionSpec as P

AXES = ("task", "dp", "mp")
SWAP = [(0, 1), (1, 0)]
EPS = 1e-06


def weighted_sums(deltas, fishers, start, size):
    d = lax.dynamic_slice_in_dim(deltas, start, size, 1).astype(jnp.float32)
    f = lax.dynamic_slice_in_dim(fishers, start, size, 1).astype(jnp.float32)
    return jnp.stack([jnp.sum(f * d, axis=0), jnp.sum(f, axis=0)])


def from_everyone(values, axes):
    size = lax.axis_size(axes)
    return lax.all_to_all(jnp.broadcast_to(values[None], (size, *values.shape)), axes, 0, 0, tiled=True)


def shards(deltas, fishers):
    deltas, fishers = jnp.swapaxes(deltas, 1, 2), jnp.swapaxes(fishers, 1, 2)
    held, columns, _ = deltas.shape
    half = columns // 2
    task = lax.axis_index("task")
    sent = weighted_sums(deltas, fishers, (1 - task) * half, half)
    received = lax.ppermute(sent, "task", SWAP)
    own = weighted_sums(deltas, fishers, task * half, half)
    wide = deltas.astype(jnp.float32)
    task_sums = jnp.sum(wide * wide, axis=(1, 2))
    total = own + received
    merged = total[0] / total[1]
    merged_sum = jnp.sum(merged * merged)
    other = lax.ppermute(merged, "task", SWAP)
    sums = from_everyone(jnp.concatenate([task_sums, merged_sum[None]]), AXES)
    sums = jnp.sum(sums.reshape(2, -1, held + 1), axis=1)
    target = jnp.mean(jnp.sqrt(sums[:, :held] + EPS))
    rescale = target / jnp.sqrt(jnp.sum(sums[:, held]) + EPS)
    low = jnp.where(task == 0, merged, other)
    high = jnp.where(task == 0, other, merged)
    return (rescale * jnp.concatenate([low, high])).T


def solution(mesh):
    placed = P("task", "dp", "mp")
    return jax.shard_map(shards, mesh=mesh, in_specs=(placed, placed), out_specs=P("dp", "mp"), check_vma=False)
```

time: 79.4 us -> 51.6 us (0.65)
  the two profiles are of different devices: /device:TPU:4 before, /device:TPU:1 now
where the time goes in v1:
time: 51.6 us; the launch traced here: 51.4 us
  waiting for transfers between devices  22.6 us (44%)
  starting transfers between devices  20.6 us (40%)
  other arithmetic  6.03 us (12%)
  between operations  1.41 us (3%)
  local copies, waits for them, and re-layouts  0.81 us (2%)
    all_to_all x1, starting transfers between devices, from_everyone(): lax.all_to_all(jnp.broadcast_to(values[None], (size, *values.shape)), axe...  17 us
    ppermute x1, waiting for transfers between devices, shards(): received = lax.ppermute(sent, 'task', SWAP)  11.4 us
    all_to_all x1, waiting for transfers between devices, from_everyone(): lax.all_to_all(jnp.broadcast_to(values[None], (size, *values.shape)), axe...  11.2 us
    ppermute x1, starting transfers between devices, shards(): received = lax.ppermute(sent, 'task', SWAP)  2.13 us
    reduce_sum x1, other arithmetic, weighted_sums(): return jnp.stack([jnp.sum(f * d, axis=0), jnp.sum(f, axis=0)])  1.89 us
    ppermute x1, starting transfers between devices, shards(): other = lax.ppermute(merged, 'task', SWAP)  1.47 us
  transfers between devices with their start and end apart: 3, of which 2 were waited for; matrix products, arithmetic and copies ran while one was open for 3% of the time, Pallas kernels for 0%

profile of v1, /device:TPU:1, one launch (start us, length us, event | category | flops | bytes accessed | tf_op | source)
XLA Modules:
  0.0 51.4 jit_solution(11760372986751925255)
XLA Ops:
  0.0 1.9 %fusion.1 = (f32[288,256]{1,0:T(8,128)S(1)}, f32[288,256]{1,0:T(8,128)S(1)}, f32[288,256]{1,0:T(8,128)S(1)}, f32[288,256]{1,0:T(8,128)S(1)}) fusion(bf16[3,256,576]{1,2,0:T(8,128)(2,1)} %param.2, s32[]{:T(128)S(6)} %select_n.20, bf16[3,256,576]{1,2,0:T(8,128)(2,1)} %param.3, s32[]{:T(128)S(6)} %select_n.21), kind=kLoop, calls=%fused_computation.5 | loop fusion | flops 1916928 | bytes 2949128 | tf_op jit(solution)/shard_map/reduce_sum | solution.py:14
  1.9 0.0 copy-start
  2.0 2.1 %collective-permute-start = (f32[2,288,256]{2,1,0:T(8,128)S(1)}, f32[2,288,256]{2,1,0:T(8,128)S(1)}, u32[]{:S(2)}, u32[]{:S(2)}) collective-permute-start(f32[2,288,256]{2,1,0:T(8,128)S(1)} %pad_maximum_fusion), channel_id=1, source_target_pairs={{0,128},{128,0},{1,129},{129,1},{2,130},{130,2},{3,131},{131,3},{4... | collective-permute-start | bytes 1769480 | tf_op jit(solution)/shard_map/ppermute | solution.py:28
  4.1 0.0 copy-done
  4.1 0.3 multiply_reduce_fusion
  4.4 11.4 %collective-permute-done = f32[2,288,256]{2,1,0:T(8,128)S(1)} collective-permute-done((f32[2,288,256]{2,1,0:T(8,128)S(1)}, f32[2,288,256]{2,1,0:T(8,128)S(1)}, u32[]{:S(2)}, u32[]{:S(2)}) %collective-permute-start) | collective-permute-done | bytes 589856 | tf_op jit(solution)/shard_map/ppermute | solution.py:28
  15.8 0.1 maximum_add_fusion
  15.9 0.7 %multiply_reduce_fusion.1 = (f32[]{:T(128)}, f32[288,256]{1,0:T(8,128)S(1)}) fusion(f32[2,288,256]{2,1,0:T(8,128)S(1)} %maximum_add_fusion), kind=kLoop, calls=%fused_computation.13 | loop fusion | flops 221183 | bytes 884740 | tf_op jit(solution)/shard_map/reduce_sum | solution.py:34
  16.6 0.7 %pad_maximum_fusion.1 = f32[4]{0:T(128)S(1)} fusion(f32[1]{0:T(128)} %bitcast.9, f32[3]{0:T(128)S(1)} %multiply_reduce_fusion), kind=kLoop, calls=%fused_computation.19 | loop fusion | flops 4 | bytes 32 | tf_op jit(solution)/shard_map/concatenate | solution.py:36
  17.3 0.7 %broadcast_in_dim.10 = f32[256,1,4]{2,1,0:T(1,128)} broadcast(f32[4]{0:T(128)S(1)} %pad_maximum_fusion.1), dimensions={2} | broadcast | bytes 4112 | tf_op jit(solution)/shard_map/broadcast_in_dim | solution.py:19
  18.0 17.0 %all-to-all-start = ((f32[256,1,4]{2,1,0:T(1,128)}), f32[256,1,4]{2,1,0:T(1,128)S(1)}, u32[]{:S(2)}, u32[]{:S(2)}) async-start(f32[256,1,4]{2,1,0:T(1,128)} %broadcast_in_dim.10), calls=%async_computation | async-start | bytes 262144 | tf_op jit(solution)/shard_map/all_to_all | solution.py:19
  35.0 1.5 %collective-permute-start.1 = (f32[288,256]{1,0:T(8,128)S(1)}, f32[288,256]{1,0:T(8,128)S(1)}, u32[]{:S(2)}, u32[]{:S(2)}) collective-permute-start(f32[288,256]{1,0:T(8,128)S(1)} %get-tuple-element.10), channel_id=1, source_target_pairs={{0,128},{128,0},{1,129},{129,1},{2,130},{130,2},{3,131},{131,3},{4... | collective-permute-start | bytes 884744 | tf_op jit(solution)/shard_map/ppermute | solution.py:35
  36.5 11.2 %all-to-all-done = f32[256,1,4]{2,1,0:T(1,128)S(1)} async-done(((f32[256,1,4]{2,1,0:T(1,128)}), f32[256,1,4]{2,1,0:T(1,128)S(1)}, u32[]{:S(2)}, u32[]{:S(2)}) %all-to-all-start) | async-done | bytes 4128 | tf_op jit(solution)/shard_map/all_to_all | solution.py:19
  47.7 0.1 copy.5
  47.7 0.1 bitcast_reduce_fusion.2
  47.8 0.7 %slice_reduce_fusion = f32[]{:T(128)} fusion(f32[2,4]{1,0:T(2,128)S(1)} %bitcast_reduce_fusion.2), kind=kLoop, calls=%fused_computation.17 | loop fusion | flops 1 | bytes 12 | tf_op jit(solution)/shard_map/reduce_sum | solution.py:39
  49.2 0.6 %sqrt_reduce_fusion = f32[]{:T(128)} fusion(f32[2,4]{1,0:T(2,128)S(1)} %bitcast_reduce_fusion.2), kind=kLoop, calls=%fused_computation.18 | loop fusion | flops 11 | bytes 28 | tf_op jit(solution)/shard_map/reduce_sum | solution.py:38
  50.5 0.0 collective-permute-done.1
  50.5 0.9 %fusion.2 = f32[256,576]{0,1:T(8,128)} fusion(f32[288,256]{1,0:T(8,128)S(1)} %get-tuple-element.12, f32[288,256]{1,0:T(8,128)S(1)} %get-tuple-element.11, f32[]{:T(128)S(6)} %div.15), kind=kLoop, calls=%fused_computation.10 | loop fusion | flops 294912 | bytes 1179652 | tf_op jit(solution)/shard_map/transpose | solution.py:42
  (2 shorter events, 0.1 us)
Async XLA Ops:
  1.9 2.2 %copy-start = (bf16[3,256,576]{1,2,0:T(8,128)(2,1)S(1)}, bf16[3,256,576]{1,2,0:T(8,128)(2,1)}, u32[]{:S(2)}) copy-start(bf16[3,256,576]{1,2,0:T(8,128)(2,1)} %param.2) | copy-start | bytes 2654212
  2.0 13.8 %collective-permute-start = (f32[2,288,256]{2,1,0:T(8,128)S(1)}, f32[2,288,256]{2,1,0:T(8,128)S(1)}, u32[]{:S(2)}, u32[]{:S(2)}) collective-permute-start(f32[2,288,256]{2,1,0:T(8,128)S(1)} %pad_maximum_fusion), channel_id=1, source_target_pairs={{0,128},{128,0},{1,129},{129,1},{2,130},{130,2},{3,131},{131,3},{4... | collective-permute-start | bytes 1769480 | tf_op jit(solution)/shard_map/ppermute | solution.py:28
  18.0 29.7 %all-to-all-start = ((f32[256,1,4]{2,1,0:T(1,128)}), f32[256,1,4]{2,1,0:T(1,128)S(1)}, u32[]{:S(2)}, u32[]{:S(2)}) async-start(f32[256,1,4]{2,1,0:T(1,128)} %broadcast_in_dim.10), calls=%async_computation | async-start | bytes 262144 | tf_op jit(solution)/shard_map/all_to_all | solution.py:19
  35.0 15.5 %collective-permute-start.1 = (f32[288,256]{1,0:T(8,128)S(1)}, f32[288,256]{1,0:T(8,128)S(1)}, u32[]{:S(2)}, u32[]{:S(2)}) collective-permute-start(f32[288,256]{1,0:T(8,128)S(1)} %get-tuple-element.10), channel_id=1, source_target_pairs={{0,128},{128,0},{1,129},{129,1},{2,130},{130,2},{3,131},{131,3},{4... | collective-permute-start | bytes 884744 | tf_op jit(solution)/shard_map/ppermute | solution.py:35

commit v2 on v1

v2 whole, which is shorter than its diff:
```python
import functools

import jax
import jax.numpy as jnp
from jax import lax
from jax.experimental import pallas as pl
from jax.experimental.pallas import tpu as pltpu
from jax.sharding import PartitionSpec as P

AXES = ("task", "dp", "mp")
SWAP = [(0, 1), (1, 0)]
EPS = 1e-06
LANES = 128
PIECES = 3
SMALL = pltpu.CompilerParams(vmem_limit_bytes=16 * 1024 * 1024)


def whole():
    return pl.BlockSpec(memory_space=pltpu.VMEM)


def hbm():
    return pl.BlockSpec(memory_space=pltpu.HBM)


def fetches(d_hbm, f_hbm, d_ref, f_ref, sems, start, at, size):
    pairs = []
    for k in range(d_hbm.shape[0]):
        pairs.append(tuple(
            pltpu.make_async_copy(src.at[k, pl.ds(start, size), :], dst.at[k, pl.ds(at, size), :], sems.at[2 * k + i])
            for i, (src, dst) in enumerate(((d_hbm, d_ref), (f_hbm, f_ref)))
        ))
    return pairs


def add_weighted(pairs, d_ref, f_ref, sums_ref):
    _, rows, _ = sums_ref.shape
    for k, pair in enumerate(pairs):
        for copy in pair:
            copy.wait()
        d = d_ref[k, :rows, :].astype(jnp.float32)
        f = f_ref[k, :rows, :].astype(jnp.float32)
        if k == 0:
            sums_ref[0], sums_ref[1] = f * d, f
        else:
            sums_ref[0] += f * d
            sums_ref[1] += f


def send_kernel(d_hbm, f_hbm, sums_ref, d_ref, f_ref, sems):
    _, rows, _ = sums_ref.shape
    start = pl.multiple_of((1 - lax.axis_index("task")) * rows, 32)
    pairs = fetches(d_hbm, f_hbm, d_ref, f_ref, sems, start, 0, rows)
    for pair in pairs:
        for copy in pair:
            copy.start()
    add_weighted(pairs, d_ref, f_ref, sums_ref)


def own_kernel(d_hbm, f_hbm, sums_ref, squares_ref, d_ref, f_ref, sems, rest_sems):
    _, rows, _ = sums_ref.shape
    held, both, columns = d_hbm.shape
    task = lax.axis_index("task")
    pairs = fetches(d_hbm, f_hbm, d_ref, f_ref, sems, pl.multiple_of(task * rows, 32), 0, rows)
    for pair in pairs:
        for copy in pair:
            copy.start()
    start = pl.multiple_of((1 - task) * rows, 32)
    rest = [
        pltpu.make_async_copy(
            d_hbm.at[k, pl.ds(start, rows), :], d_ref.at[k, pl.ds(rows, rows), :], rest_sems.at[k]
        )
        for k in range(held)
    ]
    for copy in rest:
        copy.start()
    add_weighted(pairs, d_ref, f_ref, sums_ref)
    for k in range(held):
        rest[k].wait()
        d = d_ref[k].astype(jnp.float32)
        part = jnp.sum((d * d).reshape(both // 8, 8, columns), axis=0)
        squares_ref[k] = part[:, :LANES] + part[:, LANES:]


def merge_kernel(own_ref, got_ref, squares_ref, merged_ref, message_ref):
    _, rows, columns = own_ref.shape
    merged = (own_ref[0] + got_ref[0]) / (own_ref[1] + got_ref[1])
    merged_ref[...] = merged
    part = jnp.sum((merged * merged).reshape(rows // 8, 8, columns), axis=0)
    merged_sum = jnp.sum(part, keepdims=True)
    held = squares_ref.shape[0]
    lane = lax.broadcasted_iota(jnp.int32, (1, LANES), 1)
    first = lax.axis_index("task") * held
    message = jnp.where(lane == 2 * held, merged_sum, 0.0)
    for k in range(held):
        message = jnp.where(lane == first + k, jnp.sum(squares_ref[k], keepdims=True), message)
    message_ref[...] = jnp.broadcast_to(message, message_ref.shape)


def scale_kernel(tasks, messages_ref, merged_ref, other_ref, out_hbm, scaled_ref, sems):
    rows, _ = merged_ref.shape
    sums = jnp.sum(messages_ref[...], axis=0, keepdims=True)
    lane = lax.broadcasted_iota(jnp.int32, sums.shape, 1)
    target = jnp.sum(jnp.where(lane < tasks, jnp.sqrt(sums + EPS), 0.0), keepdims=True) / tasks
    merged_sq = jnp.sum(jnp.where(lane == tasks, sums, 0.0), keepdims=True)
    rescale = target / jnp.sqrt(merged_sq + EPS)
    task = lax.axis_index("task")
    size = rows // PIECES
    copies = []
    for i, (half_ref, side) in enumerate(((merged_ref, task), (other_ref, 1 - task))):
        for j in range(PIECES):
            at = (i * PIECES + j) * size
            scaled_ref[at : at + size, :] = rescale * half_ref[j * size : (j + 1) * size, :]
            to = pl.multiple_of(side * rows + j * size, 8)
            copies.append(pltpu.make_async_copy(
                scaled_ref.at[at : at + size, :], out_hbm.at[pl.ds(to, size), :], sems.at[i * PIECES + j]
            ))
            copies[-1].start()
    for copy in copies:
        copy.wait()


def shards(deltas, fishers):
    deltas, fishers = jnp.swapaxes(deltas, 1, 2), jnp.swapaxes(fishers, 1, 2)
    deltas = pltpu.with_memory_space_constraint(deltas, pltpu.HBM)
    fishers = pltpu.with_memory_space_constraint(fishers, pltpu.HBM)
    held, columns, rows = deltas.shape
    half = columns // 2
    tasks, devices = held * lax.axis_size("task"), lax.axis_size(AXES)
    sums_type = jax.ShapeDtypeStruct((2, half, rows), jnp.float32)
    half_type = jax.ShapeDtypeStruct((half, rows), jnp.float32)
    half_input = pltpu.VMEM((held, half, rows), deltas.dtype)
    sent = pl.pallas_call(
        send_kernel, out_shape=sums_type, in_specs=[hbm()] * 2, out_specs=whole(), compiler_params=SMALL,
        scratch_shapes=[half_input, half_input, pltpu.SemaphoreType.DMA((2 * held,))],
    )(deltas, fishers)
    received = lax.ppermute(sent, "task", SWAP)
    own, squares = pl.pallas_call(
        own_kernel, out_shape=(sums_type, jax.ShapeDtypeStruct((held, 8, LANES), jnp.float32)),
        in_specs=[hbm()] * 2, out_specs=(whole(), whole()), compiler_params=SMALL,
        scratch_shapes=[
            pltpu.VMEM((held, columns, rows), deltas.dtype), half_input,
            pltpu.SemaphoreType.DMA((2 * held,)), pltpu.SemaphoreType.DMA((held,)),
        ],
    )(deltas, fishers)
    merged, message = pl.pallas_call(
        merge_kernel, out_shape=(half_type, jax.ShapeDtypeStruct((devices, LANES), jnp.float32)),
        in_specs=[whole()] * 3, out_specs=(whole(), whole()), compiler_params=SMALL,
    )(own, received, squares)
    other = lax.ppermute(merged, "task", SWAP)
    messages = lax.all_to_all(message, AXES, 0, 0, tiled=True)
    out = pl.pallas_call(
        functools.partial(scale_kernel, tasks), out_shape=jax.ShapeDtypeStruct((columns, rows), jnp.float32),
        in_specs=[whole()] * 3, out_specs=hbm(), compiler_params=SMALL,
        scratch_shapes=[pltpu.VMEM((columns, rows), jnp.float32), pltpu.SemaphoreType.DMA((2 * PIECES,))],
    )(messages, merged, other)
    return out.T


def solution(mesh):
    placed = P("task", "dp", "mp")
    return jax.shard_map(shards, mesh=mesh, in_specs=(placed, placed), out_specs=P("dp", "mp"), check_vma=False)
```

time: 51.6 us -> 47.5 us (0.921)
  blocking collectives: 0 us -> 28.5 us
  starting transfers between devices: 20.6 us -> 4.41 us
  waiting for transfers between devices: 22.6 us -> 10.1 us
  other arithmetic: 6.03 us -> 0 us
  Pallas kernels: 0 us -> 4.24 us
  between operations: 1.41 us -> 0.03 us
  local copies, waits for them, and re-layouts: 0.81 us -> 0 us
    all_to_all x0 -> x1, blocking collectives: none -> 28.5 us  [shards(): messages = lax.all_to_all(message, AXES, 0, 0, tiled=True)]
    all_to_all x1 -> x0, starting transfers between devices: 17 us -> none  [from_everyone(): lax.all_to_all(jnp.broadcast_to(values[None], (size, *values.shape)), axe...]
    all_to_all x1 -> x0, waiting for transfers between devices: 11.2 us -> none  [from_everyone(): lax.all_to_all(jnp.broadcast_to(values[None], (size, *values.shape)), axe...]
    reduce_sum x6 -> x0, other arithmetic: 4.29 us -> none  [the longest x1 1.89 us: weighted_sums(): return jnp.stack([jnp.sum(f * d, axis=0), jnp.sum(f, axis=0)])]
    pallas_call x0 -> x4, Pallas kernels: none -> 4.24 us  [the longest x1 1.6 us: shards(): pl.pallas_call(own_kernel, out_shape=(sums_type, jax.ShapeDtypeStruct((he...]
    ppermute x1, waiting for transfers between devices: 11.4 us -> 10.1 us  [shards(): received = lax.ppermute(sent, 'task', SWAP)]
    transpose x1 -> x0, other arithmetic: 0.86 us -> none  [shards(): return (rescale * jnp.concatenate([low, high])).T]
    ppermute x1, starting transfers between devices: 1.47 us -> 2.29 us  [shards(): other = lax.ppermute(merged, 'task', SWAP)]
  transfers between devices with their start and end apart: 3 -> 2, of which waited for: 2 -> 1; matrix products, arithmetic and copies ran while one was open for 3% -> 0% of each run, Pallas kernels for 0% -> 3%
where the time goes in v2:
time: 47.5 us; the launch traced here: 47.3 us
  blocking collectives  28.5 us (60%)
  waiting for transfers between devices  10.1 us (21%)
  starting transfers between devices  4.41 us (9%)
  Pallas kernels  4.24 us (9%)
    all_to_all x1, blocking collectives, shards(): messages = lax.all_to_all(message, AXES, 0, 0, tiled=True)  28.5 us
    ppermute x1, waiting for transfers between devices, shards(): received = lax.ppermute(sent, 'task', SWAP)  10.1 us
    ppermute x1, starting transfers between devices, shards(): other = lax.ppermute(merged, 'task', SWAP)  2.29 us
    ppermute x1, starting transfers between devices, shards(): received = lax.ppermute(sent, 'task', SWAP)  2.13 us
    pallas_call x1, Pallas kernels, shards(): pl.pallas_call(own_kernel, out_shape=(sums_type, jax.ShapeDtypeStruct((he...  1.6 us
    pallas_call x1, Pallas kernels, shards(): pl.pallas_call(send_kernel, out_shape=sums_type, in_specs=[hbm()] * 2, ou...  1.37 us
    pallas_call x1, Pallas kernels, shards(): pl.pallas_call(functools.partial(scale_kernel, tasks), out_shape=jax.Shap...  1.04 us
  transfers between devices with their start and end apart: 2, of which 1 were waited for; matrix products, arithmetic and copies ran while one was open for 0% of the time, Pallas kernels for 3%

profile of v2, /device:TPU:1, one launch (start us, length us, event | category | flops | bytes accessed | tf_op | source)
XLA Modules:
  0.0 47.3 jit_solution(13840050683002915069)
XLA Ops:
  0.0 1.4 %shard_map.29 = f32[2,288,256]{2,1,0:T(8,128)S(1)} custom-call(bf16[3,576,256]{2,1,0:T(8,128)(2,1)} %bitcast.9, bf16[3,576,256]{2,1,0:T(8,128)(2,1)} %bitcast.11), custom_call_target="tpu_custom_call" | custom-call | tf_op jit(solution)/shard_map/pallas_call | solution.py:133
  1.4 2.1 %collective-permute-start = (f32[2,288,256]{2,1,0:T(8,128)S(1)}, f32[2,288,256]{2,1,0:T(8,128)S(1)}, u32[]{:S(2)}, u32[]{:S(2)}) collective-permute-start(f32[2,288,256]{2,1,0:T(8,128)S(1)} %shard_map.29), channel_id=1, source_target_pairs={{0,128},{128,0},{1,129},{129,1},{2,130},{130,2},{3,131},{131,3},{4... | collective-permute-start | bytes 1769480 | tf_op jit(solution)/shard_map/ppermute | solution.py:137
  3.5 1.6 %shard_map.28 = (f32[2,288,256]{2,1,0:T(8,128)S(1)}, f32[3,8,128]{2,1,0:T(8,128)S(1)}) custom-call(bf16[3,576,256]{2,1,0:T(8,128)(2,1)} %bitcast.10, bf16[3,576,256]{2,1,0:T(8,128)(2,1)} %bitcast.12), custom_call_target="tpu_custom_call" | custom-call | tf_op jit(solution)/shard_map/pallas_call | solution.py:138
  5.1 10.1 %collective-permute-done.got_ref = f32[2,288,256]{2,1,0:T(8,128)S(1)} collective-permute-done((f32[2,288,256]{2,1,0:T(8,128)S(1)}, f32[2,288,256]{2,1,0:T(8,128)S(1)}, u32[]{:S(2)}, u32[]{:S(2)}) %collective-permute-start) | collective-permute-done | bytes 589856 | tf_op jit(solution)/shard_map/ppermute | solution.py:137
  15.2 0.2 shard_map.30
  15.4 2.3 %collective-permute-start.1 = (f32[288,256]{1,0:T(8,128)S(1)}, f32[288,256]{1,0:T(8,128)S(1)}, u32[]{:S(2)}, u32[]{:S(2)}) collective-permute-start(f32[288,256]{1,0:T(8,128)S(1)} %get-tuple-element.12.merged_ref), channel_id=1, source_target_pairs={{0,128},{128,0},{1,129},{129,1},{2,130},{130,2},{3,131},{131,3},{4... | collective-permute-start | bytes 884744 | tf_op jit(solution)/shard_map/ppermute | solution.py:150
  17.7 28.5 %all_to_all.11 = f32[256,1,128]{2,1,0:T(1,128)S(1)} all-to-all(f32[256,1,128]{2,1,0:T(1,128)S(1)} %bitcast.8), channel_id=1, replica_groups=mesh['task'=2,'dp'=16,'mp'=8] {'task','dp','mp'}, dimensions={0} | all-to-all | bytes 262144 | tf_op jit(solution)/shard_map/all_to_all | solution.py:151
  46.3 0.0 collective-permute-done.1.other_ref
  46.3 1.0 %shard_map.31 = f32[576,256]{1,0:T(8,128)} custom-call(f32[256,128]{1,0:T(8,128)S(1)} %bitcast.7, f32[288,256]{1,0:T(8,128)S(1)} %get-tuple-element.12.merged_ref, f32[288,256]{1,0:T(8,128)S(1)} %collective-permute-done.1.other_ref), custom_call_target="tpu_custom_call" | custom-call | tf_op jit(solution)/shard_map/pallas_call | solution.py:152
Async XLA Ops:
  1.4 13.8 %collective-permute-start = (f32[2,288,256]{2,1,0:T(8,128)S(1)}, f32[2,288,256]{2,1,0:T(8,128)S(1)}, u32[]{:S(2)}, u32[]{:S(2)}) collective-permute-start(f32[2,288,256]{2,1,0:T(8,128)S(1)} %shard_map.29), channel_id=1, source_target_pairs={{0,128},{128,0},{1,129},{129,1},{2,130},{130,2},{3,131},{131,3},{4... | collective-permute-start | bytes 1769480 | tf_op jit(solution)/shard_map/ppermute | solution.py:137
  15.4 30.8 %collective-permute-start.1 = (f32[288,256]{1,0:T(8,128)S(1)}, f32[288,256]{1,0:T(8,128)S(1)}, u32[]{:S(2)}, u32[]{:S(2)}) collective-permute-start(f32[288,256]{1,0:T(8,128)S(1)} %get-tuple-element.12.merged_ref), channel_id=1, source_target_pairs={{0,128},{128,0},{1,129},{129,1},{2,130},{130,2},{3,131},{131,3},{4... | collective-permute-start | bytes 884744 | tf_op jit(solution)/shard_map/ppermute | solution.py:150

commit v3 on v2

--- a/solution.py
+++ b/solution.py
@@ -12,6 +12,7 @@
 EPS = 1e-06
 LANES = 128
 PIECES = 3
+FIRST = (2, 2, 4)
 SMALL = pltpu.CompilerParams(vmem_limit_bytes=16 * 1024 * 1024)
 
 
@@ -94,7 +95,7 @@
     message = jnp.where(lane == 2 * held, merged_sum, 0.0)
     for k in range(held):
         message = jnp.where(lane == first + k, jnp.sum(squares_ref[k], keepdims=True), message)
-    message_ref[...] = jnp.broadcast_to(message, message_ref.shape)
+    message_ref[...] = message
 
 
 def scale_kernel(tasks, messages_ref, merged_ref, other_ref, out_hbm, scaled_ref, sems):
@@ -118,6 +119,21 @@
             copies[-1].start()
     for copy in copies:
         copy.wait()
+
+
+def groups_by_core(root):
+    groups = []
+    for core in range(2):
+        places = []
+        for task in range(2):
+            for z in range(8):
+                for x_hi in range(2):
+                    for y in range(4):
+                        place = (2 * x_hi + task, y, z)
+                        index = ((task * 8 + z) * 2 + core) * 8 + x_hi * 4 + y
+                        places.append((place != root, index))
+        groups.append([index for _, index in sorted(places)])
+    return groups
 
 
 def shards(deltas, fishers):
@@ -144,11 +160,14 @@
         ],
     )(deltas, fishers)
     merged, message = pl.pallas_call(
-        merge_kernel, out_shape=(half_type, jax.ShapeDtypeStruct((devices, LANES), jnp.float32)),
+        merge_kernel, out_shape=(half_type, jax.ShapeDtypeStruct((1, LANES), jnp.float32)),
         in_specs=[whole()] * 3, out_specs=(whole(), whole()), compiler_params=SMALL,
     )(own, received, squares)
     other = lax.ppermute(merged, "task", SWAP)
-    messages = lax.all_to_all(message, AXES, 0, 0, tiled=True)
+    message += lax.ppermute(message, "dp", [(i, i ^ 1) for i in range(lax.axis_size("dp"))])
+    messages = lax.all_to_all(
+        jnp.broadcast_to(message, (devices // 2, LANES)), AXES, 0, 0, tiled=True, axis_index_groups=groups_by_core(FIRST)
+    )
     out = pl.pallas_call(
         functools.partial(scale_kernel, tasks), out_shape=jax.ShapeDtypeStruct((columns, rows), jnp.float32),
         in_specs=[whole()] * 3, out_specs=hbm(), compiler_params=SMALL,

time: 47.5 us -> 39.9 us (0.84)
  blocking collectives: 28.5 us -> 19.1 us
  starting transfers between devices: 4.41 us -> 6.27 us
    all_to_all x1, blocking collectives: 28.5 us -> 19.1 us  [shards(): lax.all_to_all(jnp.broadcast_to(message, (devices // 2, LANES)), AXES, 0,...]
    ppermute x0 -> x1, starting transfers between devices: none -> 2.66 us  [shards(): lax.ppermute(message, 'dp', [(i, i ^ 1) for i in range(lax.axis_size('dp'...]
    ppermute x1, starting transfers between devices: 2.29 us -> 1.48 us  [shards(): other = lax.ppermute(merged, 'task', SWAP)]
  transfers between devices with their start and end apart: 2 -> 3, of which waited for: 1 -> 1; matrix products, arithmetic and copies ran while one was open for 0% -> 0% of each run, Pallas kernels for 3% -> 4%
where the time goes in v3:
time: 39.9 us; the launch traced here: 39.7 us
  blocking collectives  19.1 us (48%)
  waiting for transfers between devices  10.1 us (25%)
  starting transfers between devices  6.27 us (16%)
  Pallas kernels  4.2 us (11%)
    all_to_all x1, blocking collectives, shards(): lax.all_to_all(jnp.broadcast_to(message, (devices // 2, LANES)), AXES, 0,...  19.1 us
    ppermute x1, waiting for transfers between devices, shards(): received = lax.ppermute(sent, 'task', SWAP)  10.1 us
    ppermute x1, starting transfers between devices, shards(): lax.ppermute(message, 'dp', [(i, i ^ 1) for i in range(lax.axis_size('dp'...  2.66 us
    ppermute x1, starting transfers between devices, shards(): received = lax.ppermute(sent, 'task', SWAP)  2.13 us
    pallas_call x1, Pallas kernels, shards(): pl.pallas_call(own_kernel, out_shape=(sums_type, jax.ShapeDtypeStruct((he...  1.6 us
    ppermute x1, starting transfers between devices, shards(): other = lax.ppermute(merged, 'task', SWAP)  1.48 us
    pallas_call x1, Pallas kernels, shards(): pl.pallas_call(send_kernel, out_shape=sums_type, in_specs=[hbm()] * 2, ou...  1.37 us
    pallas_call x1, Pallas kernels, shards(): pl.pallas_call(functools.partial(scale_kernel, tasks), out_shape=jax.Shap...  1.03 us
  transfers between devices with their start and end apart: 3, of which 1 were waited for; matrix products, arithmetic and copies ran while one was open for 0% of the time, Pallas kernels for 4%

profile of v3, /device:TPU:1, one launch (start us, length us, event | category | flops | bytes accessed | tf_op | source)
XLA Modules:
  0.0 39.7 jit_solution(9929243788602437673)
XLA Ops:
  0.0 1.4 %shard_map.29 = f32[2,288,256]{2,1,0:T(8,128)S(1)} custom-call(bf16[3,576,256]{2,1,0:T(8,128)(2,1)} %bitcast.7, bf16[3,576,256]{2,1,0:T(8,128)(2,1)} %bitcast.9), custom_call_target="tpu_custom_call" | custom-call | tf_op jit(solution)/shard_map/pallas_call | solution.py:149
  1.4 2.1 %collective-permute-start = (f32[2,288,256]{2,1,0:T(8,128)S(1)}, f32[2,288,256]{2,1,0:T(8,128)S(1)}, u32[]{:S(2)}, u32[]{:S(2)}) collective-permute-start(f32[2,288,256]{2,1,0:T(8,128)S(1)} %shard_map.29), channel_id=1, source_target_pairs={{0,128},{128,0},{1,129},{129,1},{2,130},{130,2},{3,131},{131,3},{4... | collective-permute-start | bytes 1769480 | tf_op jit(solution)/shard_map/ppermute | solution.py:153
  3.5 1.6 %shard_map.28 = (f32[2,288,256]{2,1,0:T(8,128)S(1)}, f32[3,8,128]{2,1,0:T(8,128)S(1)}) custom-call(bf16[3,576,256]{2,1,0:T(8,128)(2,1)} %bitcast.8, bf16[3,576,256]{2,1,0:T(8,128)(2,1)} %bitcast.10), custom_call_target="tpu_custom_call" | custom-call | tf_op jit(solution)/shard_map/pallas_call | solution.py:154
  5.1 10.1 %collective-permute-done.got_ref = f32[2,288,256]{2,1,0:T(8,128)S(1)} collective-permute-done((f32[2,288,256]{2,1,0:T(8,128)S(1)}, f32[2,288,256]{2,1,0:T(8,128)S(1)}, u32[]{:S(2)}, u32[]{:S(2)}) %collective-permute-start) | collective-permute-done | bytes 589856 | tf_op jit(solution)/shard_map/ppermute | solution.py:153
  15.2 0.2 shard_map.30
  15.4 2.7 %collective-permute-start.1 = (f32[1,128]{1,0:T(1,128)S(1)}, f32[1,128]{1,0:T(1,128)S(1)}, u32[]{:S(2)}, u32[]{:S(2)}) collective-permute-start(f32[1,128]{1,0:T(1,128)S(1)} %get-tuple-element.11), channel_id=1, source_target_pairs={{0,8},{8,0},{16,24},{24,16},{32,40},{40,32},{48,56},{56,48},{64,72... | collective-permute-start | bytes 1544 | tf_op jit(solution)/shard_map/ppermute | solution.py:167
  18.1 1.5 %collective-permute-start.2 = (f32[288,256]{1,0:T(8,128)S(1)}, f32[288,256]{1,0:T(8,128)S(1)}, u32[]{:S(2)}, u32[]{:S(2)}) collective-permute-start(f32[288,256]{1,0:T(8,128)S(1)} %get-tuple-element.12.merged_ref), channel_id=1, source_target_pairs={{0,128},{128,0},{1,129},{129,1},{2,130},{130,2},{3,131},{131,3},{4... | collective-permute-start | bytes 884744 | tf_op jit(solution)/shard_map/ppermute | solution.py:166
  19.6 0.0 collective-permute-done.1
  19.6 19.1 %all_to_all.8 = f32[128,1,128]{2,1,0:T(1,128)S(1)} all-to-all(f32[128,1,128]{2,1,0:T(1,128)S(1)} %broadcast_in_dim.2), channel_id=1, replica_groups={{70,0,1,2,3,4,5,6,7,16,17,18,19,20,21,22,23,32,33,34,35,36,37,38,39,48,..., dimensions={0} | all-to-all | bytes 131072 | tf_op jit(solution)/shard_map/all_to_all | solution.py:168
  38.7 0.0 collective-permute-done.2.other_ref
  38.7 1.0 %shard_map.31 = f32[576,256]{1,0:T(8,128)} custom-call(f32[128,128]{1,0:T(8,128)S(1)} %bitcast.6, f32[288,256]{1,0:T(8,128)S(1)} %get-tuple-element.12.merged_ref, f32[288,256]{1,0:T(8,128)S(1)} %collective-permute-done.2.other_ref), custom_call_target="tpu_custom_call" | custom-call | tf_op jit(solution)/shard_map/pallas_call | solution.py:171
  (2 shorter events, 0.0 us)
Async XLA Ops:
  1.4 13.8 %collective-permute-start = (f32[2,288,256]{2,1,0:T(8,128)S(1)}, f32[2,288,256]{2,1,0:T(8,128)S(1)}, u32[]{:S(2)}, u32[]{:S(2)}) collective-permute-start(f32[2,288,256]{2,1,0:T(8,128)S(1)} %shard_map.29), channel_id=1, source_target_pairs={{0,128},{128,0},{1,129},{129,1},{2,130},{130,2},{3,131},{131,3},{4... | collective-permute-start | bytes 1769480 | tf_op jit(solution)/shard_map/ppermute | solution.py:153
  15.4 4.1 %collective-permute-start.1 = (f32[1,128]{1,0:T(1,128)S(1)}, f32[1,128]{1,0:T(1,128)S(1)}, u32[]{:S(2)}, u32[]{:S(2)}) collective-permute-start(f32[1,128]{1,0:T(1,128)S(1)} %get-tuple-element.11), channel_id=1, source_target_pairs={{0,8},{8,0},{16,24},{24,16},{32,40},{40,32},{48,56},{56,48},{64,72... | collective-permute-start | bytes 1544 | tf_op jit(solution)/shard_map/ppermute | solution.py:167
  18.1 20.6 %collective-permute-start.2 = (f32[288,256]{1,0:T(8,128)S(1)}, f32[288,256]{1,0:T(8,128)S(1)}, u32[]{:S(2)}, u32[]{:S(2)}) collective-permute-start(f32[288,256]{1,0:T(8,128)S(1)} %get-tuple-element.12.merged_ref), channel_id=1, source_target_pairs={{0,128},{128,0},{1,129},{129,1},{2,130},{130,2},{3,131},{131,3},{4... | collective-permute-start | bytes 884744 | tf_op jit(solution)/shard_map/ppermute | solution.py:166

commit v4 on v3

--- a/solution.py
+++ b/solution.py
@@ -11,8 +11,9 @@
 SWAP = [(0, 1), (1, 0)]
 EPS = 1e-06
 LANES = 128
+EARLY = 64
 PIECES = 3
-FIRST = (2, 2, 4)
+FIRST = (2, 2, 5)
 SMALL = pltpu.CompilerParams(vmem_limit_bytes=16 * 1024 * 1024)
 
 
@@ -48,14 +49,26 @@
             sums_ref[1] += f
 
 
-def send_kernel(d_hbm, f_hbm, sums_ref, d_ref, f_ref, sems):
+def send_kernel(skip, d_hbm, f_hbm, sums_ref, d_ref, f_ref, sems):
     _, rows, _ = sums_ref.shape
-    start = pl.multiple_of((1 - lax.axis_index("task")) * rows, 32)
-    pairs = fetches(d_hbm, f_hbm, d_ref, f_ref, sems, start, 0, rows)
-    for pair in pairs:
-        for copy in pair:
-            copy.start()
-    add_weighted(pairs, d_ref, f_ref, sums_ref)
+    half = d_hbm.shape[1] // 2
+    start = pl.multiple_of((1 - lax.axis_index("task")) * half + skip, 32)
+    copies = [
+        pltpu.make_async_copy(src.at[:, pl.ds(start, rows), :], dst, sems.at[i])
+        for i, (src, dst) in enumerate(((d_hbm, d_ref), (f_hbm, f_ref)))
+    ]
+    for copy in copies:
+        copy.start()
+    for copy in copies:
+        copy.wait()
+
+    @pl.loop(0, rows // 32)
+    def _(i):
+        at = pl.ds(pl.multiple_of(i * 32, 32), 32)
+        d = d_ref[:, at, :].astype(jnp.float32)
+        f = f_ref[:, at, :].astype(jnp.float32)
+        sums_ref[0, at, :] = jnp.sum(f * d, axis=0)
+        sums_ref[1, at, :] = jnp.sum(f, axis=0)
 
 
 def own_kernel(d_hbm, f_hbm, sums_ref, squares_ref, d_ref, f_ref, sems, rest_sems):
@@ -83,11 +96,16 @@
         squares_ref[k] = part[:, :LANES] + part[:, LANES:]
 
 
-def merge_kernel(own_ref, got_ref, squares_ref, merged_ref, message_ref):
-    _, rows, columns = own_ref.shape
-    merged = (own_ref[0] + got_ref[0]) / (own_ref[1] + got_ref[1])
-    merged_ref[...] = merged
-    part = jnp.sum((merged * merged).reshape(rows // 8, 8, columns), axis=0)
+def merge_kernel(own_ref, first_ref, rest_ref, squares_ref, merged_ref, message_ref):
+    columns = own_ref.shape[2]
+    at, part = 0, 0.0
+    for got_ref in (first_ref, rest_ref):
+        rows = got_ref.shape[1]
+        own = own_ref[:, at : at + rows, :]
+        merged = (own[0] + got_ref[0]) / (own[1] + got_ref[1])
+        merged_ref[at : at + rows, :] = merged
+        part += jnp.sum((merged * merged).reshape(rows // 8, 8, columns), axis=0)
+        at += rows
     merged_sum = jnp.sum(part, keepdims=True)
     held = squares_ref.shape[0]
     lane = lax.broadcasted_iota(jnp.int32, (1, LANES), 1)
@@ -146,11 +164,15 @@
     sums_type = jax.ShapeDtypeStruct((2, half, rows), jnp.float32)
     half_type = jax.ShapeDtypeStruct((half, rows), jnp.float32)
     half_input = pltpu.VMEM((held, half, rows), deltas.dtype)
-    sent = pl.pallas_call(
-        send_kernel, out_shape=sums_type, in_specs=[hbm()] * 2, out_specs=whole(), compiler_params=SMALL,
-        scratch_shapes=[half_input, half_input, pltpu.SemaphoreType.DMA((2 * held,))],
-    )(deltas, fishers)
-    received = lax.ppermute(sent, "task", SWAP)
+    received = []
+    for skip, size in ((0, EARLY), (EARLY, half - EARLY)):
+        part_input = pltpu.VMEM((held, size, rows), deltas.dtype)
+        sent = pl.pallas_call(
+            functools.partial(send_kernel, skip), out_shape=jax.ShapeDtypeStruct((2, size, rows), jnp.float32),
+            in_specs=[hbm()] * 2, out_specs=whole(), compiler_params=SMALL,
+            scratch_shapes=[part_input, part_input, pltpu.SemaphoreType.DMA((2,))],
+        )(deltas, fishers)
+        received.append(lax.ppermute(sent, "task", SWAP))
     own, squares = pl.pallas_call(
         own_kernel, out_shape=(sums_type, jax.ShapeDtypeStruct((held, 8, LANES), jnp.float32)),
         in_specs=[hbm()] * 2, out_specs=(whole(), whole()), compiler_params=SMALL,
@@ -161,8 +183,8 @@
     )(deltas, fishers)
     merged, message = pl.pallas_call(
         merge_kernel, out_shape=(half_type, jax.ShapeDtypeStruct((1, LANES), jnp.float32)),
-        in_specs=[whole()] * 3, out_specs=(whole(), whole()), compiler_params=SMALL,
-    )(own, received, squares)
+        in_specs=[whole()] * 4, out_specs=(whole(), whole()), compiler_params=SMALL,
+    )(own, *received, squares)
     other = lax.ppermute(merged, "task", SWAP)
     message += lax.ppermute(message, "dp", [(i, i ^ 1) for i in range(lax.axis_size("dp"))])
     messages = lax.all_to_all(

time: 39.9 us -> 39.6 us (level)
  waiting for transfers between devices: 10.1 us -> 8.99 us
  Pallas kernels: 4.2 us -> 5.04 us
    ppermute x1 -> x2, waiting for transfers between devices: 10.1 us -> 8.99 us  [shards(): received.append(lax.ppermute(sent, 'task', SWAP))]
    pallas_call x1 -> x2, Pallas kernels: 1.37 us -> 2.2 us  [shards(): pl.pallas_call(functools.partial(send_kernel, skip), out_shape=jax.ShapeD...]
    ppermute x1 -> x2, starting transfers between devices: 2.13 us -> 2.24 us  [shards(): received.append(lax.ppermute(sent, 'task', SWAP))]
  transfers between devices with their start and end apart: 3 -> 4, of which waited for: 1 -> 1; matrix products, arithmetic and copies ran while one was open for 0% -> 0% of each run, Pallas kernels for 4% -> 7%
where the time goes in v4:
time: 39.6 us; the launch traced here: 39.4 us
  blocking collectives  18.9 us (48%)
  waiting for transfers between devices  8.99 us (23%)
  starting transfers between devices  6.38 us (16%)
  Pallas kernels  5.04 us (13%)
    all_to_all x1, blocking collectives, shards(): lax.all_to_all(jnp.broadcast_to(message, (devices // 2, LANES)), AXES, 0,...  18.9 us
    ppermute x2, waiting for transfers between devices, shards(): received.append(lax.ppermute(sent, 'task', SWAP))  8.99 us
    ppermute x1, starting transfers between devices, shards(): lax.ppermute(message, 'dp', [(i, i ^ 1) for i in range(lax.axis_size('dp'...  2.66 us
    ppermute x2, starting transfers between devices, shards(): received.append(lax.ppermute(sent, 'task', SWAP))  2.24 us
    pallas_call x2, Pallas kernels, shards(): pl.pallas_call(functools.partial(send_kernel, skip), out_shape=jax.ShapeD...  2.2 us
    pallas_call x1, Pallas kernels, shards(): pl.pallas_call(own_kernel, out_shape=(sums_type, jax.ShapeDtypeStruct((he...  1.6 us
    ppermute x1, starting transfers between devices, shards(): other = lax.ppermute(merged, 'task', SWAP)  1.48 us
    pallas_call x1, Pallas kernels, shards(): pl.pallas_call(functools.partial(scale_kernel, tasks), out_shape=jax.Shap...  1.03 us
  transfers between devices with their start and end apart: 4, of which 1 were waited for; matrix products, arithmetic and copies ran while one was open for 0% of the time, Pallas kernels for 7%

profile of v4, /device:TPU:1, one launch (start us, length us, event | category | flops | bytes accessed | tf_op | source)
XLA Modules:
  0.0 39.4 jit_solution(976038946103303893)
XLA Ops:
  0.0 1.2 %shard_map.30 = f32[2,224,256]{2,1,0:T(8,128)S(1)} custom-call(bf16[3,576,256]{2,1,0:T(8,128)(2,1)} %bitcast.7, bf16[3,576,256]{2,1,0:T(8,128)(2,1)} %bitcast.10), custom_call_target="tpu_custom_call" | custom-call | tf_op jit(solution)/shard_map/pallas_call | solution.py:170
  1.2 2.1 %collective-permute-start.1 = (f32[2,224,256]{2,1,0:T(8,128)S(1)}, f32[2,224,256]{2,1,0:T(8,128)S(1)}, u32[]{:S(2)}, u32[]{:S(2)}) collective-permute-start(f32[2,224,256]{2,1,0:T(8,128)S(1)} %shard_map.30), channel_id=1, source_target_pairs={{0,128},{128,0},{1,129},{129,1},{2,130},{130,2},{3,131},{131,3},{4... | collective-permute-start | bytes 1376264 | tf_op jit(solution)/shard_map/ppermute | solution.py:175
  3.4 1.0 %shard_map.29 = f32[2,64,256]{2,1,0:T(8,128)S(1)} custom-call(bf16[3,576,256]{2,1,0:T(8,128)(2,1)} %bitcast.8, bf16[3,576,256]{2,1,0:T(8,128)(2,1)} %bitcast.11), custom_call_target="tpu_custom_call" | custom-call | tf_op jit(solution)/shard_map/pallas_call | solution.py:170
  4.3 0.1 collective-permute-start
  4.5 1.6 %shard_map.28 = (f32[2,288,256]{2,1,0:T(8,128)S(1)}, f32[3,8,128]{2,1,0:T(8,128)S(1)}) custom-call(bf16[3,576,256]{2,1,0:T(8,128)(2,1)} %bitcast.9, bf16[3,576,256]{2,1,0:T(8,128)(2,1)} %bitcast.12), custom_call_target="tpu_custom_call" | custom-call | tf_op jit(solution)/shard_map/pallas_call | solution.py:176
  6.1 9.0 %collective-permute-done.first_ref = f32[2,64,256]{2,1,0:T(8,128)S(1)} collective-permute-done((f32[2,64,256]{2,1,0:T(8,128)S(1)}, f32[2,64,256]{2,1,0:T(8,128)S(1)}, u32[]{:S(2)}, u32[]{:S(2)}) %collective-permute-start) | collective-permute-done | bytes 131104 | tf_op jit(solution)/shard_map/ppermute | solution.py:175
  15.1 0.0 collective-permute-done.1.rest_ref
  15.1 0.2 shard_map.31
  15.3 2.7 %collective-permute-start.2 = (f32[1,128]{1,0:T(1,128)S(1)}, f32[1,128]{1,0:T(1,128)S(1)}, u32[]{:S(2)}, u32[]{:S(2)}) collective-permute-start(f32[1,128]{1,0:T(1,128)S(1)} %get-tuple-element.11), channel_id=1, source_target_pairs={{0,8},{8,0},{16,24},{24,16},{32,40},{40,32},{48,56},{56,48},{64,72... | collective-permute-start | bytes 1544 | tf_op jit(solution)/shard_map/ppermute | solution.py:189
  17.9 1.5 %collective-permute-start.3 = (f32[288,256]{1,0:T(8,128)S(1)}, f32[288,256]{1,0:T(8,128)S(1)}, u32[]{:S(2)}, u32[]{:S(2)}) collective-permute-start(f32[288,256]{1,0:T(8,128)S(1)} %get-tuple-element.12.merged_ref), channel_id=1, source_target_pairs={{0,128},{128,0},{1,129},{129,1},{2,130},{130,2},{3,131},{131,3},{4... | collective-permute-start | bytes 884744 | tf_op jit(solution)/shard_map/ppermute | solution.py:188
  19.4 0.0 collective-permute-done.2
  19.5 18.9 %all_to_all.8 = f32[128,1,128]{2,1,0:T(1,128)S(1)} all-to-all(f32[128,1,128]{2,1,0:T(1,128)S(1)} %broadcast_in_dim.2), channel_id=1, replica_groups={{86,0,1,2,3,4,5,6,7,16,17,18,19,20,21,22,23,32,33,34,35,36,37,38,39,48,..., dimensions={0} | all-to-all | bytes 131072 | tf_op jit(solution)/shard_map/all_to_all | solution.py:190
  38.4 0.0 collective-permute-done.3.other_ref
  38.4 1.0 %shard_map.32 = f32[576,256]{1,0:T(8,128)} custom-call(f32[128,128]{1,0:T(8,128)S(1)} %bitcast.6, f32[288,256]{1,0:T(8,128)S(1)} %get-tuple-element.12.merged_ref, f32[288,256]{1,0:T(8,128)S(1)} %collective-permute-done.3.other_ref), custom_call_target="tpu_custom_call" | custom-call | tf_op jit(solution)/shard_map/pallas_call | solution.py:193
  (2 shorter events, 0.0 us)
Async XLA Ops:
  1.2 13.8 %collective-permute-start.1 = (f32[2,224,256]{2,1,0:T(8,128)S(1)}, f32[2,224,256]{2,1,0:T(8,128)S(1)}, u32[]{:S(2)}, u32[]{:S(2)}) collective-permute-start(f32[2,224,256]{2,1,0:T(8,128)S(1)} %shard_map.30), channel_id=1, source_target_pairs={{0,128},{128,0},{1,129},{129,1},{2,130},{130,2},{3,131},{131,3},{4... | collective-permute-start | bytes 1376264 | tf_op jit(solution)/shard_map/ppermute | solution.py:175
  4.3 10.7 %collective-permute-start = (f32[2,64,256]{2,1,0:T(8,128)S(1)}, f32[2,64,256]{2,1,0:T(8,128)S(1)}, u32[]{:S(2)}, u32[]{:S(2)}) collective-permute-start(f32[2,64,256]{2,1,0:T(8,128)S(1)} %shard_map.29), channel_id=1, source_target_pairs={{0,128},{128,0},{1,129},{129,1},{2,130},{130,2},{3,131},{131,3},{4... | collective-permute-start | bytes 393224 | tf_op jit(solution)/shard_map/ppermute | solution.py:175
  15.3 4.1 %collective-permute-start.2 = (f32[1,128]{1,0:T(1,128)S(1)}, f32[1,128]{1,0:T(1,128)S(1)}, u32[]{:S(2)}, u32[]{:S(2)}) collective-permute-start(f32[1,128]{1,0:T(1,128)S(1)} %get-tuple-element.11), channel_id=1, source_target_pairs={{0,8},{8,0},{16,24},{24,16},{32,40},{40,32},{48,56},{56,48},{64,72... | collective-permute-start | bytes 1544 | tf_op jit(solution)/shard_map/ppermute | solution.py:189
  17.9 20.5 %collective-permute-start.3 = (f32[288,256]{1,0:T(8,128)S(1)}, f32[288,256]{1,0:T(8,128)S(1)}, u32[]{:S(2)}, u32[]{:S(2)}) collective-permute-start(f32[288,256]{1,0:T(8,128)S(1)} %get-tuple-element.12.merged_ref), channel_id=1, source_target_pairs={{0,128},{128,0},{1,129},{129,1},{2,130},{130,2},{3,131},{131,3},{4... | collective-permute-start | bytes 884744 | tf_op jit(solution)/shard_map/ppermute | solution.py:188

commit v5 on v4

--- a/solution.py
+++ b/solution.py
@@ -11,7 +11,7 @@
 SWAP = [(0, 1), (1, 0)]
 EPS = 1e-06
 LANES = 128
-EARLY = 64
+PARTS = ((0, 96), (96, 96), (192, 96))
 PIECES = 3
 FIRST = (2, 2, 5)
 SMALL = pltpu.CompilerParams(vmem_limit_bytes=16 * 1024 * 1024)
@@ -96,10 +96,11 @@
         squares_ref[k] = part[:, :LANES] + part[:, LANES:]
 
 
-def merge_kernel(own_ref, first_ref, rest_ref, squares_ref, merged_ref, message_ref):
+def merge_kernel(own_ref, *refs):
+    *got_refs, squares_ref, merged_ref, message_ref = refs
     columns = own_ref.shape[2]
     at, part = 0, 0.0
-    for got_ref in (first_ref, rest_ref):
+    for got_ref in got_refs:
         rows = got_ref.shape[1]
         own = own_ref[:, at : at + rows, :]
         merged = (own[0] + got_ref[0]) / (own[1] + got_ref[1])
@@ -165,7 +166,7 @@
     half_type = jax.ShapeDtypeStruct((half, rows), jnp.float32)
     half_input = pltpu.VMEM((held, half, rows), deltas.dtype)
     received = []
-    for skip, size in ((0, EARLY), (EARLY, half - EARLY)):
+    for skip, size in PARTS:
         part_input = pltpu.VMEM((held, size, rows), deltas.dtype)
         sent = pl.pallas_call(
             functools.partial(send_kernel, skip), out_shape=jax.ShapeDtypeStruct((2, size, rows), jnp.float32),
@@ -183,7 +184,7 @@
     )(deltas, fishers)
     merged, message = pl.pallas_call(
         merge_kernel, out_shape=(half_type, jax.ShapeDtypeStruct((1, LANES), jnp.float32)),
-        in_specs=[whole()] * 4, out_specs=(whole(), whole()), compiler_params=SMALL,
+        in_specs=[whole()] * (2 + len(PARTS)), out_specs=(whole(), whole()), compiler_params=SMALL,
     )(own, *received, squares)
     other = lax.ppermute(merged, "task", SWAP)
     message += lax.ppermute(message, "dp", [(i, i ^ 1) for i in range(lax.axis_size("dp"))])

time: 39.6 us -> 39.5 us (level)
  waiting for transfers between devices: 8.99 us -> 6.46 us
  starting transfers between devices: 6.38 us -> 7.79 us
  Pallas kernels: 5.04 us -> 5.97 us
    ppermute x2 -> x3, waiting for transfers between devices: 8.99 us -> 6.46 us  [shards(): received.append(lax.ppermute(sent, 'task', SWAP))]
    ppermute x2 -> x3, starting transfers between devices: 2.24 us -> 3.77 us  [shards(): received.append(lax.ppermute(sent, 'task', SWAP))]
    pallas_call x2 -> x3, Pallas kernels: 2.2 us -> 3.14 us  [shards(): pl.pallas_call(functools.partial(send_kernel, skip), out_shape=jax.ShapeD...]
    ppermute x1, starting transfers between devices: 1.48 us -> 0.98 us  [shards(): other = lax.ppermute(merged, 'task', SWAP)]
  transfers between devices with their start and end apart: 4 -> 5, of which waited for: 1 -> 2; matrix products, arithmetic and copies ran while one was open for 0% -> 0% of each run, Pallas kernels for 7% -> 9%
where the time goes in v5:
time: 39.5 us; the launch traced here: 39.3 us
  blocking collectives  18.9 us (48%)
  starting transfers between devices  7.79 us (20%)
  waiting for transfers between devices  6.46 us (16%)
  Pallas kernels  5.97 us (15%)
    all_to_all x1, blocking collectives, shards(): lax.all_to_all(jnp.broadcast_to(message, (devices // 2, LANES)), AXES, 0,...  18.9 us
    ppermute x3, waiting for transfers between devices, shards(): received.append(lax.ppermute(sent, 'task', SWAP))  6.46 us
    ppermute x3, starting transfers between devices, shards(): received.append(lax.ppermute(sent, 'task', SWAP))  3.77 us
    pallas_call x3, Pallas kernels, shards(): pl.pallas_call(functools.partial(send_kernel, skip), out_shape=jax.ShapeD...  3.14 us
    ppermute x1, starting transfers between devices, shards(): lax.ppermute(message, 'dp', [(i, i ^ 1) for i in range(lax.axis_size('dp'...  3.04 us
    pallas_call x1, Pallas kernels, shards(): pl.pallas_call(own_kernel, out_shape=(sums_type, jax.ShapeDtypeStruct((he...  1.6 us
    pallas_call x1, Pallas kernels, shards(): pl.pallas_call(functools.partial(scale_kernel, tasks), out_shape=jax.Shap...  1.03 us
    ppermute x1, starting transfers between devices, shards(): other = lax.ppermute(merged, 'task', SWAP)  0.98 us
  transfers between devices with their start and end apart: 5, of which 2 were waited for; matrix products, arithmetic and copies ran while one was open for 0% of the time, Pallas kernels for 9%

profile of v5, /device:TPU:1, one launch (start us, length us, event | category | flops | bytes accessed | tf_op | source)
XLA Modules:
  0.0 39.3 jit_solution(17010411097171164326)
XLA Ops:
  0.0 1.0 %shard_map.29 = f32[2,96,256]{2,1,0:T(8,128)S(1)} custom-call(bf16[3,576,256]{2,1,0:T(8,128)(2,1)} %bitcast.7, bf16[3,576,256]{2,1,0:T(8,128)(2,1)} %bitcast.11), custom_call_target="tpu_custom_call" | custom-call | tf_op jit(solution)/shard_map/pallas_call | solution.py:171
  1.1 2.1 %collective-permute-start = (f32[2,96,256]{2,1,0:T(8,128)S(1)}, f32[2,96,256]{2,1,0:T(8,128)S(1)}, u32[]{:S(2)}, u32[]{:S(2)}) collective-permute-start(f32[2,96,256]{2,1,0:T(8,128)S(1)} %shard_map.29), channel_id=1, source_target_pairs={{0,128},{128,0},{1,129},{129,1},{2,130},{130,2},{3,131},{131,3},{4... | collective-permute-start | bytes 589832 | tf_op jit(solution)/shard_map/ppermute | solution.py:176
  3.2 1.0 %shard_map.30 = f32[2,96,256]{2,1,0:T(8,128)S(1)} custom-call(bf16[3,576,256]{2,1,0:T(8,128)(2,1)} %bitcast.8, bf16[3,576,256]{2,1,0:T(8,128)(2,1)} %bitcast.12), custom_call_target="tpu_custom_call" | custom-call | tf_op jit(solution)/shard_map/pallas_call | solution.py:171
  4.2 0.1 collective-permute-start.1
  4.4 1.0 %shard_map.31 = f32[2,96,256]{2,1,0:T(8,128)S(1)} custom-call(bf16[3,576,256]{2,1,0:T(8,128)(2,1)} %bitcast.9, bf16[3,576,256]{2,1,0:T(8,128)(2,1)} %bitcast.13), custom_call_target="tpu_custom_call" | custom-call | tf_op jit(solution)/shard_map/pallas_call | solution.py:171
  5.4 1.5 %collective-permute-start.2 = (f32[2,96,256]{2,1,0:T(8,128)S(1)}, f32[2,96,256]{2,1,0:T(8,128)S(1)}, u32[]{:S(2)}, u32[]{:S(2)}) collective-permute-start(f32[2,96,256]{2,1,0:T(8,128)S(1)} %shard_map.31), channel_id=1, source_target_pairs={{0,128},{128,0},{1,129},{129,1},{2,130},{130,2},{3,131},{131,3},{4... | collective-permute-start | bytes 589832 | tf_op jit(solution)/shard_map/ppermute | solution.py:176
  6.9 1.6 %shard_map.28 = (f32[2,288,256]{2,1,0:T(8,128)S(1)}, f32[3,8,128]{2,1,0:T(8,128)S(1)}) custom-call(bf16[3,576,256]{2,1,0:T(8,128)(2,1)} %bitcast.10, bf16[3,576,256]{2,1,0:T(8,128)(2,1)} %bitcast.14), custom_call_target="tpu_custom_call" | custom-call | tf_op jit(solution)/shard_map/pallas_call | solution.py:177
  8.5 0.0 collective-permute-done.refs_0_
  8.6 2.2 %collective-permute-done.1.refs_1_ = f32[2,96,256]{2,1,0:T(8,128)S(1)} collective-permute-done((f32[2,96,256]{2,1,0:T(8,128)S(1)}, f32[2,96,256]{2,1,0:T(8,128)S(1)}, u32[]{:S(2)}, u32[]{:S(2)}) %collective-permute-start.1) | collective-permute-done | bytes 196640 | tf_op jit(solution)/shard_map/ppermute | solution.py:176
  10.8 4.2 %collective-permute-done.2.refs_2_ = f32[2,96,256]{2,1,0:T(8,128)S(1)} collective-permute-done((f32[2,96,256]{2,1,0:T(8,128)S(1)}, f32[2,96,256]{2,1,0:T(8,128)S(1)}, u32[]{:S(2)}, u32[]{:S(2)}) %collective-permute-start.2) | collective-permute-done | bytes 196640 | tf_op jit(solution)/shard_map/ppermute | solution.py:176
  15.0 0.2 shard_map.32
  15.2 3.0 %collective-permute-start.3 = (f32[1,128]{1,0:T(1,128)S(1)}, f32[1,128]{1,0:T(1,128)S(1)}, u32[]{:S(2)}, u32[]{:S(2)}) collective-permute-start(f32[1,128]{1,0:T(1,128)S(1)} %get-tuple-element.11), channel_id=1, source_target_pairs={{0,8},{8,0},{16,24},{24,16},{32,40},{40,32},{48,56},{56,48},{64,72... | collective-permute-start | bytes 1544 | tf_op jit(solution)/shard_map/ppermute | solution.py:190
  18.3 1.0 %collective-permute-start.4 = (f32[288,256]{1,0:T(8,128)S(1)}, f32[288,256]{1,0:T(8,128)S(1)}, u32[]{:S(2)}, u32[]{:S(2)}) collective-permute-start(f32[288,256]{1,0:T(8,128)S(1)} %get-tuple-element.12.merged_ref), channel_id=1, source_target_pairs={{0,128},{128,0},{1,129},{129,1},{2,130},{130,2},{3,131},{131,3},{4... | collective-permute-start | bytes 884744 | tf_op jit(solution)/shard_map/ppermute | solution.py:189
  19.2 0.0 collective-permute-done.3
  19.3 18.9 %all_to_all.8 = f32[128,1,128]{2,1,0:T(1,128)S(1)} all-to-all(f32[128,1,128]{2,1,0:T(1,128)S(1)} %broadcast_in_dim.2), channel_id=1, replica_groups={{86,0,1,2,3,4,5,6,7,16,17,18,19,20,21,22,23,32,33,34,35,36,37,38,39,48,..., dimensions={0} | all-to-all | bytes 131072 | tf_op jit(solution)/shard_map/all_to_all | solution.py:191
  38.2 0.0 collective-permute-done.4.other_ref
  38.2 1.0 %shard_map.33 = f32[576,256]{1,0:T(8,128)} custom-call(f32[128,128]{1,0:T(8,128)S(1)} %bitcast.6, f32[288,256]{1,0:T(8,128)S(1)} %get-tuple-element.12.merged_ref, f32[288,256]{1,0:T(8,128)S(1)} %collective-permute-done.4.other_ref), custom_call_target="tpu_custom_call" | custom-call | tf_op jit(solution)/shard_map/pallas_call | solution.py:194
  (2 shorter events, 0.0 us)
Async XLA Ops:
  1.1 7.5 %collective-permute-start = (f32[2,96,256]{2,1,0:T(8,128)S(1)}, f32[2,96,256]{2,1,0:T(8,128)S(1)}, u32[]{:S(2)}, u32[]{:S(2)}) collective-permute-start(f32[2,96,256]{2,1,0:T(8,128)S(1)} %shard_map.29), channel_id=1, source_target_pairs={{0,128},{128,0},{1,129},{129,1},{2,130},{130,2},{3,131},{131,3},{4... | collective-permute-start | bytes 589832 | tf_op jit(solution)/shard_map/ppermute | solution.py:176
  4.2 6.6 %collective-permute-start.1 = (f32[2,96,256]{2,1,0:T(8,128)S(1)}, f32[2,96,256]{2,1,0:T(8,128)S(1)}, u32[]{:S(2)}, u32[]{:S(2)}) collective-permute-start(f32[2,96,256]{2,1,0:T(8,128)S(1)} %shard_map.30), channel_id=1, source_target_pairs={{0,128},{128,0},{1,129},{129,1},{2,130},{130,2},{3,131},{131,3},{4... | collective-permute-start | bytes 589832 | tf_op jit(solution)/shard_map/ppermute | solution.py:176
  5.4 9.6 %collective-permute-start.2 = (f32[2,96,256]{2,1,0:T(8,128)S(1)}, f32[2,96,256]{2,1,0:T(8,128)S(1)}, u32[]{:S(2)}, u32[]{:S(2)}) collective-permute-start(f32[2,96,256]{2,1,0:T(8,128)S(1)} %shard_map.31), channel_id=1, source_target_pairs={{0,128},{128,0},{1,129},{129,1},{2,130},{130,2},{3,131},{131,3},{4... | collective-permute-start | bytes 589832 | tf_op jit(solution)/shard_map/ppermute | solution.py:176
  15.2 4.0 %collective-permute-start.3 = (f32[1,128]{1,0:T(1,128)S(1)}, f32[1,128]{1,0:T(1,128)S(1)}, u32[]{:S(2)}, u32[]{:S(2)}) collective-permute-start(f32[1,128]{1,0:T(1,128)S(1)} %get-tuple-element.11), channel_id=1, source_target_pairs={{0,8},{8,0},{16,24},{24,16},{32,40},{40,32},{48,56},{56,48},{64,72... | collective-permute-start | bytes 1544 | tf_op jit(solution)/shard_map/ppermute | solution.py:190
  18.3 20.0 %collective-permute-start.4 = (f32[288,256]{1,0:T(8,128)S(1)}, f32[288,256]{1,0:T(8,128)S(1)}, u32[]{:S(2)}, u32[]{:S(2)}) collective-permute-start(f32[288,256]{1,0:T(8,128)S(1)} %get-tuple-element.12.merged_ref), channel_id=1, source_target_pairs={{0,128},{128,0},{1,129},{129,1},{2,130},{130,2},{3,131},{131,3},{4... | collective-permute-start | bytes 884744 | tf_op jit(solution)/shard_map/ppermute | solution.py:189

commit v6 on v5

--- a/solution.py
+++ b/solution.py
@@ -11,7 +11,7 @@
 SWAP = [(0, 1), (1, 0)]
 EPS = 1e-06
 LANES = 128
-PARTS = ((0, 96), (96, 96), (192, 96))
+PARTS = ((0, 64), (64, 160), (224, 64))
 PIECES = 3
 FIRST = (2, 2, 5)
 SMALL = pltpu.CompilerParams(vmem_limit_bytes=16 * 1024 * 1024)
@@ -96,8 +96,8 @@
         squares_ref[k] = part[:, :LANES] + part[:, LANES:]
 
 
-def merge_kernel(own_ref, *refs):
-    *got_refs, squares_ref, merged_ref, message_ref = refs
+def early_kernel(own_ref, *refs):
+    *got_refs, merged_ref, part_ref = refs
     columns = own_ref.shape[2]
     at, part = 0, 0.0
     for got_ref in got_refs:
@@ -107,6 +107,17 @@
         merged_ref[at : at + rows, :] = merged
         part += jnp.sum((merged * merged).reshape(rows // 8, 8, columns), axis=0)
         at += rows
+    part_ref[...] = part
+
+
+def merge_kernel(own_ref, got_ref, early_ref, part_ref, squares_ref, merged_ref, message_ref):
+    columns = own_ref.shape[2]
+    rows, at = got_ref.shape[1], early_ref.shape[0]
+    own = own_ref[:, at : at + rows, :]
+    merged = (own[0] + got_ref[0]) / (own[1] + got_ref[1])
+    merged_ref[:at, :] = early_ref[...]
+    merged_ref[at : at + rows, :] = merged
+    part = part_ref[...] + jnp.sum((merged * merged).reshape(rows // 8, 8, columns), axis=0)
     merged_sum = jnp.sum(part, keepdims=True)
     held = squares_ref.shape[0]
     lane = lax.broadcasted_iota(jnp.int32, (1, LANES), 1)
@@ -182,10 +193,17 @@
             pltpu.SemaphoreType.DMA((2 * held,)), pltpu.SemaphoreType.DMA((held,)),
         ],
     )(deltas, fishers)
+    *early_got, last = received
+    done = half - PARTS[-1][1]
+    early, part = pl.pallas_call(
+        early_kernel,
+        out_shape=(jax.ShapeDtypeStruct((done, rows), jnp.float32), jax.ShapeDtypeStruct((8, rows), jnp.float32)),
+        in_specs=[whole()] * len(PARTS), out_specs=(whole(), whole()), compiler_params=SMALL,
+    )(own, *early_got)
     merged, message = pl.pallas_call(
         merge_kernel, out_shape=(half_type, jax.ShapeDtypeStruct((1, LANES), jnp.float32)),
-        in_specs=[whole()] * (2 + len(PARTS)), out_specs=(whole(), whole()), compiler_params=SMALL,
-    )(own, *received, squares)
+        in_specs=[whole()] * 5, out_specs=(whole(), whole()), compiler_params=SMALL,
+    )(own, last, early, part, squares)
     other = lax.ppermute(merged, "task", SWAP)
     message += lax.ppermute(message, "dp", [(i, i ^ 1) for i in range(lax.axis_size("dp"))])
     messages = lax.all_to_all(

time: 39.5 us -> 39.6 us (level)
    ppermute x1, starting transfers between devices: 0.98 us -> 1.48 us  [shards(): other = lax.ppermute(merged, 'task', SWAP)]
where the time goes in v6:
time: 39.6 us; the launch traced here: 39.3 us
  blocking collectives  18.9 us (48%)
  starting transfers between devices  7.9 us (20%)
  waiting for transfers between devices  6.38 us (16%)
  Pallas kernels  6 us (15%)
    all_to_all x1, blocking collectives, shards(): lax.all_to_all(jnp.broadcast_to(message, (devices // 2, LANES)), AXES, 0,...  18.9 us
    ppermute x3, waiting for transfers between devices, shards(): received.append(lax.ppermute(sent, 'task', SWAP))  6.38 us
    ppermute x3, starting transfers between devices, shards(): received.append(lax.ppermute(sent, 'task', SWAP))  3.77 us
    pallas_call x3, Pallas kernels, shards(): pl.pallas_call(functools.partial(send_kernel, skip), out_shape=jax.ShapeD...  3.14 us
    ppermute x1, starting transfers between devices, shards(): lax.ppermute(message, 'dp', [(i, i ^ 1) for i in range(lax.axis_size('dp'...  2.66 us
    pallas_call x1, Pallas kernels, shards(): pl.pallas_call(own_kernel, out_shape=(sums_type, jax.ShapeDtypeStruct((he...  1.62 us
    ppermute x1, starting transfers between devices, shards(): other = lax.ppermute(merged, 'task', SWAP)  1.48 us
    pallas_call x1, Pallas kernels, shards(): pl.pallas_call(functools.partial(scale_kernel, tasks), out_shape=jax.Shap...  1.03 us
  transfers between devices with their start and end apart: 5, of which 2 were waited for; matrix products, arithmetic and copies ran while one was open for 0% of the time, Pallas kernels for 9%

profile of v6, /device:TPU:1, one launch (start us, length us, event | category | flops | bytes accessed | tf_op | source)
XLA Modules:
  0.0 39.3 jit_solution(2431160061941868568)
XLA Ops:
  0.0 1.2 %shard_map.31 = f32[2,160,256]{2,1,0:T(8,128)S(1)} custom-call(bf16[3,576,256]{2,1,0:T(8,128)(2,1)} %bitcast.7, bf16[3,576,256]{2,1,0:T(8,128)(2,1)} %bitcast.11), custom_call_target="tpu_custom_call" | custom-call | tf_op jit(solution)/shard_map/pallas_call | solution.py:182
  1.2 2.1 %collective-permute-start.2 = (f32[2,160,256]{2,1,0:T(8,128)S(1)}, f32[2,160,256]{2,1,0:T(8,128)S(1)}, u32[]{:S(2)}, u32[]{:S(2)}) collective-permute-start(f32[2,160,256]{2,1,0:T(8,128)S(1)} %shard_map.31), channel_id=1, source_target_pairs={{0,128},{128,0},{1,129},{129,1},{2,130},{130,2},{3,131},{131,3},{4... | collective-permute-start | bytes 983048 | tf_op jit(solution)/shard_map/ppermute | solution.py:187
  3.3 1.0 %shard_map.30 = f32[2,64,256]{2,1,0:T(8,128)S(1)} custom-call(bf16[3,576,256]{2,1,0:T(8,128)(2,1)} %bitcast.8, bf16[3,576,256]{2,1,0:T(8,128)(2,1)} %bitcast.12), custom_call_target="tpu_custom_call" | custom-call | tf_op jit(solution)/shard_map/pallas_call | solution.py:182
  4.3 0.1 collective-permute-start.1
  4.4 1.0 %shard_map.29 = f32[2,64,256]{2,1,0:T(8,128)S(1)} custom-call(bf16[3,576,256]{2,1,0:T(8,128)(2,1)} %bitcast.9, bf16[3,576,256]{2,1,0:T(8,128)(2,1)} %bitcast.13), custom_call_target="tpu_custom_call" | custom-call | tf_op jit(solution)/shard_map/pallas_call | solution.py:182
  5.4 1.5 %collective-permute-start = (f32[2,64,256]{2,1,0:T(8,128)S(1)}, f32[2,64,256]{2,1,0:T(8,128)S(1)}, u32[]{:S(2)}, u32[]{:S(2)}) collective-permute-start(f32[2,64,256]{2,1,0:T(8,128)S(1)} %shard_map.29), channel_id=1, source_target_pairs={{0,128},{128,0},{1,129},{129,1},{2,130},{130,2},{3,131},{131,3},{4... | collective-permute-start | bytes 393224 | tf_op jit(solution)/shard_map/ppermute | solution.py:187
  6.9 1.6 %shard_map.28 = (f32[2,288,256]{2,1,0:T(8,128)S(1)}, f32[3,8,128]{2,1,0:T(8,128)S(1)}) custom-call(bf16[3,576,256]{2,1,0:T(8,128)(2,1)} %bitcast.10, bf16[3,576,256]{2,1,0:T(8,128)(2,1)} %bitcast.14), custom_call_target="tpu_custom_call" | custom-call | tf_op jit(solution)/shard_map/pallas_call | solution.py:188
  8.6 3.6 %collective-permute-done.1.refs_0_ = f32[2,64,256]{2,1,0:T(8,128)S(1)} collective-permute-done((f32[2,64,256]{2,1,0:T(8,128)S(1)}, f32[2,64,256]{2,1,0:T(8,128)S(1)}, u32[]{:S(2)}, u32[]{:S(2)}) %collective-permute-start.1) | collective-permute-done | bytes 131104 | tf_op jit(solution)/shard_map/ppermute | solution.py:187
  12.2 0.0 collective-permute-done.2.refs_1_
  12.2 0.1 shard_map.32
  12.3 2.7 %collective-permute-done.got_ref = f32[2,64,256]{2,1,0:T(8,128)S(1)} collective-permute-done((f32[2,64,256]{2,1,0:T(8,128)S(1)}, f32[2,64,256]{2,1,0:T(8,128)S(1)}, u32[]{:S(2)}, u32[]{:S(2)}) %collective-permute-start) | collective-permute-done | bytes 131104 | tf_op jit(solution)/shard_map/ppermute | solution.py:187
  15.0 0.2 shard_map.33
  15.2 2.7 %collective-permute-start.3 = (f32[1,128]{1,0:T(1,128)S(1)}, f32[1,128]{1,0:T(1,128)S(1)}, u32[]{:S(2)}, u32[]{:S(2)}) collective-permute-start(f32[1,128]{1,0:T(1,128)S(1)} %get-tuple-element.15), channel_id=1, source_target_pairs={{0,8},{8,0},{16,24},{24,16},{32,40},{40,32},{48,56},{56,48},{64,72... | collective-permute-start | bytes 1544 | tf_op jit(solution)/shard_map/ppermute | solution.py:208
  17.8 1.5 %collective-permute-start.4 = (f32[288,256]{1,0:T(8,128)S(1)}, f32[288,256]{1,0:T(8,128)S(1)}, u32[]{:S(2)}, u32[]{:S(2)}) collective-permute-start(f32[288,256]{1,0:T(8,128)S(1)} %get-tuple-element.16.merged_ref), channel_id=1, source_target_pairs={{0,128},{128,0},{1,129},{129,1},{2,130},{130,2},{3,131},{131,3},{4... | collective-permute-start | bytes 884744 | tf_op jit(solution)/shard_map/ppermute | solution.py:207
  19.3 0.0 collective-permute-done.3
  19.4 18.9 %all_to_all.8 = f32[128,1,128]{2,1,0:T(1,128)S(1)} all-to-all(f32[128,1,128]{2,1,0:T(1,128)S(1)} %broadcast_in_dim.2), channel_id=1, replica_groups={{86,0,1,2,3,4,5,6,7,16,17,18,19,20,21,22,23,32,33,34,35,36,37,38,39,48,..., dimensions={0} | all-to-all | bytes 131072 | tf_op jit(solution)/shard_map/all_to_all | solution.py:209
  38.3 0.0 collective-permute-done.4.other_ref
  38.3 1.0 %shard_map.34 = f32[576,256]{1,0:T(8,128)} custom-call(f32[128,128]{1,0:T(8,128)S(1)} %bitcast.6, f32[288,256]{1,0:T(8,128)S(1)} %get-tuple-element.16.merged_ref, f32[288,256]{1,0:T(8,128)S(1)} %collective-permute-done.4.other_ref), custom_call_target="tpu_custom_call" | custom-call | tf_op jit(solution)/shard_map/pallas_call | solution.py:212
  (2 shorter events, 0.0 us)
Async XLA Ops:
  1.2 11.0 %collective-permute-start.2 = (f32[2,160,256]{2,1,0:T(8,128)S(1)}, f32[2,160,256]{2,1,0:T(8,128)S(1)}, u32[]{:S(2)}, u32[]{:S(2)}) collective-permute-start(f32[2,160,256]{2,1,0:T(8,128)S(1)} %shard_map.31), channel_id=1, source_target_pairs={{0,128},{128,0},{1,129},{129,1},{2,130},{130,2},{3,131},{131,3},{4... | collective-permute-start | bytes 983048 | tf_op jit(solution)/shard_map/ppermute | solution.py:187
  4.3 7.9 %collective-permute-start.1 = (f32[2,64,256]{2,1,0:T(8,128)S(1)}, f32[2,64,256]{2,1,0:T(8,128)S(1)}, u32[]{:S(2)}, u32[]{:S(2)}) collective-permute-start(f32[2,64,256]{2,1,0:T(8,128)S(1)} %shard_map.30), channel_id=1, source_target_pairs={{0,128},{128,0},{1,129},{129,1},{2,130},{130,2},{3,131},{131,3},{4... | collective-permute-start | bytes 393224 | tf_op jit(solution)/shard_map/ppermute | solution.py:187
  5.4 9.6 %collective-permute-start = (f32[2,64,256]{2,1,0:T(8,128)S(1)}, f32[2,64,256]{2,1,0:T(8,128)S(1)}, u32[]{:S(2)}, u32[]{:S(2)}) collective-permute-start(f32[2,64,256]{2,1,0:T(8,128)S(1)} %shard_map.29), channel_id=1, source_target_pairs={{0,128},{128,0},{1,129},{129,1},{2,130},{130,2},{3,131},{131,3},{4... | collective-permute-start | bytes 393224 | tf_op jit(solution)/shard_map/ppermute | solution.py:187
  15.2 4.1 %collective-permute-start.3 = (f32[1,128]{1,0:T(1,128)S(1)}, f32[1,128]{1,0:T(1,128)S(1)}, u32[]{:S(2)}, u32[]{:S(2)}) collective-permute-start(f32[1,128]{1,0:T(1,128)S(1)} %get-tuple-element.15), channel_id=1, source_target_pairs={{0,8},{8,0},{16,24},{24,16},{32,40},{40,32},{48,56},{56,48},{64,72... | collective-permute-start | bytes 1544 | tf_op jit(solution)/shard_map/ppermute | solution.py:208
  17.8 20.5 %collective-permute-start.4 = (f32[288,256]{1,0:T(8,128)S(1)}, f32[288,256]{1,0:T(8,128)S(1)}, u32[]{:S(2)}, u32[]{:S(2)}) collective-permute-start(f32[288,256]{1,0:T(8,128)S(1)} %get-tuple-element.16.merged_ref), channel_id=1, source_target_pairs={{0,128},{128,0},{1,129},{129,1},{2,130},{130,2},{3,131},{131,3},{4... | collective-permute-start | bytes 884744 | tf_op jit(solution)/shard_map/ppermute | solution.py:207

commit v7 on v6

--- a/solution.py
+++ b/solution.py
@@ -11,7 +11,7 @@
 SWAP = [(0, 1), (1, 0)]
 EPS = 1e-06
 LANES = 128
-PARTS = ((0, 64), (64, 160), (224, 64))
+PARTS = ((0, 96), (96, 160), (256, 32))
 PIECES = 3
 FIRST = (2, 2, 5)
 SMALL = pltpu.CompilerParams(vmem_limit_bytes=16 * 1024 * 1024)

time: 39.6 us -> 39.6 us (level)
  no operation moved by 1% of the time
where the time goes in v7:
time: 39.6 us; the launch traced here: 39.3 us
  blocking collectives  18.9 us (48%)
  starting transfers between devices  7.9 us (20%)
  waiting for transfers between devices  6.45 us (16%)
  Pallas kernels  5.93 us (15%)
    all_to_all x1, blocking collectives, shards(): lax.all_to_all(jnp.broadcast_to(message, (devices // 2, LANES)), AXES, 0,...  18.9 us
    ppermute x3, waiting for transfers between devices, shards(): received.append(lax.ppermute(sent, 'task', SWAP))  6.45 us
    ppermute x3, starting transfers between devices, shards(): received.append(lax.ppermute(sent, 'task', SWAP))  3.77 us
    pallas_call x3, Pallas kernels, shards(): pl.pallas_call(functools.partial(send_kernel, skip), out_shape=jax.ShapeD...  3.06 us
    ppermute x1, starting transfers between devices, shards(): lax.ppermute(message, 'dp', [(i, i ^ 1) for i in range(lax.axis_size('dp'...  2.66 us
    pallas_call x1, Pallas kernels, shards(): pl.pallas_call(own_kernel, out_shape=(sums_type, jax.ShapeDtypeStruct((he...  1.62 us
    ppermute x1, starting transfers between devices, shards(): other = lax.ppermute(merged, 'task', SWAP)  1.48 us
    pallas_call x1, Pallas kernels, shards(): pl.pallas_call(functools.partial(scale_kernel, tasks), out_shape=jax.Shap...  1.03 us
  transfers between devices with their start and end apart: 5, of which 2 were waited for; matrix products, arithmetic and copies ran while one was open for 0% of the time, Pallas kernels for 9%

profile of v7, /device:TPU:1, one launch (start us, length us, event | category | flops | bytes accessed | tf_op | source)
XLA Modules:
  0.0 39.3 jit_solution(16613873271888350828)
XLA Ops:
  0.0 1.2 %shard_map.31 = f32[2,160,256]{2,1,0:T(8,128)S(1)} custom-call(bf16[3,576,256]{2,1,0:T(8,128)(2,1)} %bitcast.7, bf16[3,576,256]{2,1,0:T(8,128)(2,1)} %bitcast.11), custom_call_target="tpu_custom_call" | custom-call | tf_op jit(solution)/shard_map/pallas_call | solution.py:182
  1.2 2.1 %collective-permute-start.2 = (f32[2,160,256]{2,1,0:T(8,128)S(1)}, f32[2,160,256]{2,1,0:T(8,128)S(1)}, u32[]{:S(2)}, u32[]{:S(2)}) collective-permute-start(f32[2,160,256]{2,1,0:T(8,128)S(1)} %shard_map.31), channel_id=1, source_target_pairs={{0,128},{128,0},{1,129},{129,1},{2,130},{130,2},{3,131},{131,3},{4... | collective-permute-start | bytes 983048 | tf_op jit(solution)/shard_map/ppermute | solution.py:187
  3.3 1.0 %shard_map.30 = f32[2,96,256]{2,1,0:T(8,128)S(1)} custom-call(bf16[3,576,256]{2,1,0:T(8,128)(2,1)} %bitcast.8, bf16[3,576,256]{2,1,0:T(8,128)(2,1)} %bitcast.12), custom_call_target="tpu_custom_call" | custom-call | tf_op jit(solution)/shard_map/pallas_call | solution.py:182
  4.3 0.1 collective-permute-start.1
  4.5 0.9 %shard_map.29 = f32[2,32,256]{2,1,0:T(8,128)S(1)} custom-call(bf16[3,576,256]{2,1,0:T(8,128)(2,1)} %bitcast.9, bf16[3,576,256]{2,1,0:T(8,128)(2,1)} %bitcast.13), custom_call_target="tpu_custom_call" | custom-call | tf_op jit(solution)/shard_map/pallas_call | solution.py:182
  5.3 1.5 %collective-permute-start = (f32[2,32,256]{2,1,0:T(8,128)S(1)}, f32[2,32,256]{2,1,0:T(8,128)S(1)}, u32[]{:S(2)}, u32[]{:S(2)}) collective-permute-start(f32[2,32,256]{2,1,0:T(8,128)S(1)} %shard_map.29), channel_id=1, source_target_pairs={{0,128},{128,0},{1,129},{129,1},{2,130},{130,2},{3,131},{131,3},{4... | collective-permute-start | bytes 196616 | tf_op jit(solution)/shard_map/ppermute | solution.py:187
  6.9 1.6 %shard_map.28 = (f32[2,288,256]{2,1,0:T(8,128)S(1)}, f32[3,8,128]{2,1,0:T(8,128)S(1)}) custom-call(bf16[3,576,256]{2,1,0:T(8,128)(2,1)} %bitcast.10, bf16[3,576,256]{2,1,0:T(8,128)(2,1)} %bitcast.14), custom_call_target="tpu_custom_call" | custom-call | tf_op jit(solution)/shard_map/pallas_call | solution.py:188
  8.5 5.1 %collective-permute-done.1.refs_0_ = f32[2,96,256]{2,1,0:T(8,128)S(1)} collective-permute-done((f32[2,96,256]{2,1,0:T(8,128)S(1)}, f32[2,96,256]{2,1,0:T(8,128)S(1)}, u32[]{:S(2)}, u32[]{:S(2)}) %collective-permute-start.1) | collective-permute-done | bytes 196640 | tf_op jit(solution)/shard_map/ppermute | solution.py:187
  13.6 0.0 collective-permute-done.2.refs_1_
  13.6 0.1 shard_map.32
  13.7 1.3 %collective-permute-done.got_ref = f32[2,32,256]{2,1,0:T(8,128)S(1)} collective-permute-done((f32[2,32,256]{2,1,0:T(8,128)S(1)}, f32[2,32,256]{2,1,0:T(8,128)S(1)}, u32[]{:S(2)}, u32[]{:S(2)}) %collective-permute-start) | collective-permute-done | bytes 65568 | tf_op jit(solution)/shard_map/ppermute | solution.py:187
  15.0 0.1 shard_map.33
  15.2 2.7 %collective-permute-start.3 = (f32[1,128]{1,0:T(1,128)S(1)}, f32[1,128]{1,0:T(1,128)S(1)}, u32[]{:S(2)}, u32[]{:S(2)}) collective-permute-start(f32[1,128]{1,0:T(1,128)S(1)} %get-tuple-element.15), channel_id=1, source_target_pairs={{0,8},{8,0},{16,24},{24,16},{32,40},{40,32},{48,56},{56,48},{64,72... | collective-permute-start | bytes 1544 | tf_op jit(solution)/shard_map/ppermute | solution.py:208
  17.8 1.5 %collective-permute-start.4 = (f32[288,256]{1,0:T(8,128)S(1)}, f32[288,256]{1,0:T(8,128)S(1)}, u32[]{:S(2)}, u32[]{:S(2)}) collective-permute-start(f32[288,256]{1,0:T(8,128)S(1)} %get-tuple-element.16.merged_ref), channel_id=1, source_target_pairs={{0,128},{128,0},{1,129},{129,1},{2,130},{130,2},{3,131},{131,3},{4... | collective-permute-start | bytes 884744 | tf_op jit(solution)/shard_map/ppermute | solution.py:207
  19.3 0.0 collective-permute-done.3
  19.3 18.9 %all_to_all.8 = f32[128,1,128]{2,1,0:T(1,128)S(1)} all-to-all(f32[128,1,128]{2,1,0:T(1,128)S(1)} %broadcast_in_dim.2), channel_id=1, replica_groups={{86,0,1,2,3,4,5,6,7,16,17,18,19,20,21,22,23,32,33,34,35,36,37,38,39,48,..., dimensions={0} | all-to-all | bytes 131072 | tf_op jit(solution)/shard_map/all_to_all | solution.py:209
  38.3 0.0 collective-permute-done.4.other_ref
  38.3 1.0 %shard_map.34 = f32[576,256]{1,0:T(8,128)} custom-call(f32[128,128]{1,0:T(8,128)S(1)} %bitcast.6, f32[288,256]{1,0:T(8,128)S(1)} %get-tuple-element.16.merged_ref, f32[288,256]{1,0:T(8,128)S(1)} %collective-permute-done.4.other_ref), custom_call_target="tpu_custom_call" | custom-call | tf_op jit(solution)/shard_map/pallas_call | solution.py:212
  (2 shorter events, 0.0 us)
Async XLA Ops:
  1.2 12.4 %collective-permute-start.2 = (f32[2,160,256]{2,1,0:T(8,128)S(1)}, f32[2,160,256]{2,1,0:T(8,128)S(1)}, u32[]{:S(2)}, u32[]{:S(2)}) collective-permute-start(f32[2,160,256]{2,1,0:T(8,128)S(1)} %shard_map.31), channel_id=1, source_target_pairs={{0,128},{128,0},{1,129},{129,1},{2,130},{130,2},{3,131},{131,3},{4... | collective-permute-start | bytes 983048 | tf_op jit(solution)/shard_map/ppermute | solution.py:187
  4.3 9.3 %collective-permute-start.1 = (f32[2,96,256]{2,1,0:T(8,128)S(1)}, f32[2,96,256]{2,1,0:T(8,128)S(1)}, u32[]{:S(2)}, u32[]{:S(2)}) collective-permute-start(f32[2,96,256]{2,1,0:T(8,128)S(1)} %shard_map.30), channel_id=1, source_target_pairs={{0,128},{128,0},{1,129},{129,1},{2,130},{130,2},{3,131},{131,3},{4... | collective-permute-start | bytes 589832 | tf_op jit(solution)/shard_map/ppermute | solution.py:187
  5.3 9.7 %collective-permute-start = (f32[2,32,256]{2,1,0:T(8,128)S(1)}, f32[2,32,256]{2,1,0:T(8,128)S(1)}, u32[]{:S(2)}, u32[]{:S(2)}) collective-permute-start(f32[2,32,256]{2,1,0:T(8,128)S(1)} %shard_map.29), channel_id=1, source_target_pairs={{0,128},{128,0},{1,129},{129,1},{2,130},{130,2},{3,131},{131,3},{4... | collective-permute-start | bytes 196616 | tf_op jit(solution)/shard_map/ppermute | solution.py:187
  15.2 4.1 %collective-permute-start.3 = (f32[1,128]{1,0:T(1,128)S(1)}, f32[1,128]{1,0:T(1,128)S(1)}, u32[]{:S(2)}, u32[]{:S(2)}) collective-permute-start(f32[1,128]{1,0:T(1,128)S(1)} %get-tuple-element.15), channel_id=1, source_target_pairs={{0,8},{8,0},{16,24},{24,16},{32,40},{40,32},{48,56},{56,48},{64,72... | collective-permute-start | bytes 1544 | tf_op jit(solution)/shard_map/ppermute | solution.py:208
  17.8 20.5 %collective-permute-start.4 = (f32[288,256]{1,0:T(8,128)S(1)}, f32[288,256]{1,0:T(8,128)S(1)}, u32[]{:S(2)}, u32[]{:S(2)}) collective-permute-start(f32[288,256]{1,0:T(8,128)S(1)} %get-tuple-element.16.merged_ref), channel_id=1, source_target_pairs={{0,128},{128,0},{1,129},{129,1},{2,130},{130,2},{3,131},{131,3},{4... | collective-permute-start | bytes 884744 | tf_op jit(solution)/shard_map/ppermute | solution.py:207
